TPU v7x, 32 devices: a whole 2x2x4 slice. The times are simulated.
32 devices in a mesh: dp: 8 (over z, y), blk: 4 (over x, core).
Axes of the slice: x: 2, y: 2, z: 4, core: 2. Of those that a mesh axis runs over, the one named last changes fastest.
Arguments:
- features: bfloat16 [174080, 256], P('dp'), may hold values from -6 to 6
- roi_table: int32 [8, 8192], P(None, ('dp', 'blk')), may hold values from 0 to 192, as said below
- offsets: int32 [2, 32], P(None, 'dp'), may hold values from 0 to 320, as said below
- box_targets: float32 [4, 8192], P(None, ('dp', 'blk')), may hold values from -6 to 6
- first_weight: float32 [12544, 1024], P('dp', 'blk'), may hold values from -0.0546875 to 0.0546875
- first_mean: float32 [12544, 1024], P('dp', 'blk'), may hold values from -0.00048828125 to 0.00048828125
- first_square: float32 [12544, 1024], P('dp', 'blk'), may hold values from 7.6904295e-11 to 3.0517577e-10
- second_weight: float32 [1024, 1024], P('dp', 'blk'), may hold values from -0.1875 to 0.1875
- second_mean: float32 [1024, 1024], P('dp', 'blk'), may hold values from -0.00048828125 to 0.00048828125
- second_square: float32 [1024, 1024], P('dp', 'blk'), may hold values from 1.0986328e-10 to 4.394531e-10
- out_weight: float32 [1024, 85], replicated, may hold values from -0.5 to 0.5
- out_mean: float32 [1024, 85], replicated, may hold values from -0.0029296875 to 0.0029296875
- out_square: float32 [1024, 85], replicated, may hold values from 3.5400392e-09 to 1.4160157e-08
- biases: float32 [2133], replicated, may hold values from -1.5 to 1.5
- bias_mean: float32 [2133], replicated, may hold values from -0.0017089844 to 0.0017089844
- bias_square: float32 [2133], replicated, may hold values from 1.2207031e-09 to 4.8828124e-09
Outputs:
- feature_grads: float32 [174080, 256], P(('dp', 'blk'))
- total_loss: float32 [], replicated
- first_new: float32 [12544, 1024], P('dp', 'blk')
- first_mean_new: float32 [12544, 1024], P('dp', 'blk')
- first_square_new: float32 [12544, 1024], P('dp', 'blk')
- second_new: float32 [1024, 1024], P('dp', 'blk')
- second_mean_new: float32 [1024, 1024], P('dp', 'blk')
- second_square_new: float32 [1024, 1024], P('dp', 'blk')
- out_new: float32 [1024, 85], replicated
- out_mean_new: float32 [1024, 85], replicated
- out_square_new: float32 [1024, 85], replicated
- bias_new: float32 [2133], replicated
- bias_mean_new: float32 [2133], replicated
- bias_square_new: float32 [2133], replicated
Inputs may be any that keep to these rules, and one draw needn't show every extreme that they name: Rows of roi_table: left, top, right, bottom pixel edges of a box inside its image of 192 pixels a side, right > left and bottom > top; image 0 to 3 within the RoI's canvas; level 0 to 3; label 0 to 80 with 0 background; valid flag 0 or 1. `offsets`: each image of 192 pixels a side lies wholly inside its canvas, images of one canvas do not intersect.
All inputs are finite; a program needn't handle non-finite values.
Results may differ from a plain program's by a relative error of at most 0.018.
Values may be sent and summed in bfloat16 or wider, within the bound.
A program may use at most 320 MiB of HBM per device.

v0:
```python
import jax
import jax.numpy as jnp
from jax import lax
from jax.sharding import PartitionSpec as P

C = 256
H = 1024
CLASSES = 81
CANVAS = 512
IMAGES = 4
STEP = 10
K1 = 12544


third = 1.0 / 3.0
rate_first = 0.018
rate_second = 0.06
rate_out = 0.18
rate_bias = 0.2


def smooth_unit(values):
    return jax.nn.gelu(values, approximate=False)


def contract_rows(left_side, right_side):
    return lax.dot_general(
        left_side, right_side, (((0,), (0,)), ((), ())), preferred_element_type=jnp.float32
    )


def contract_cols(left_side, right_side):
    return lax.dot_general(
        left_side, right_side, (((1,), (1,)), ((), ())), preferred_element_type=jnp.float32
    )


def sample_table(roi_table, offsets):
    level_of = roi_table[5]
    image_of = roi_table[4]
    choose = (image_of[:, None] == jnp.arange(IMAGES, dtype=jnp.int32)[None, :]).astype(jnp.int32)
    shift_y = jnp.sum(choose * offsets[0][None, :], axis=1)
    shift_x = jnp.sum(choose * offsets[1][None, :], axis=1)
    grid_side = jnp.right_shift(jnp.full_like(level_of, CANVAS // 4), level_of)
    cell_base = jnp.zeros_like(level_of)
    for finer in range(1, 4):
        prior_side = CANVAS // 4 >> finer - 1
        cell_base = cell_base + jnp.where(level_of >= finer, prior_side * prior_side, 0).astype(
            jnp.int32
        )
    stride_px = (4 * jnp.left_shift(jnp.ones_like(level_of), level_of)).astype(jnp.float32)
    centres = (jnp.arange(7, dtype=jnp.float32) + 0.5) / 7.0

    def axis_points(low_edge, high_edge, shift_by):
        start_px = (low_edge + shift_by).astype(jnp.float32)
        extent = (high_edge - low_edge).astype(jnp.float32)
        points = start_px[:, None] + centres[None, :] * extent[:, None]
        limit_max = (grid_side - 1).astype(jnp.float32)[:, None]
        scaled = jnp.clip(points / stride_px[:, None] - 0.5, 0.0, limit_max)
        floor_idx = jnp.minimum(jnp.floor(scaled).astype(jnp.int32), grid_side[:, None] - 2)
        return (floor_idx, scaled - floor_idx.astype(jnp.float32))

    row_low, row_frac = axis_points(roi_table[1], roi_table[3], shift_y)
    col_low, col_frac = axis_points(roi_table[0], roi_table[2], shift_x)
    index_list = []
    weight_list = []
    for corner_row in (0, 1):
        for corner_col in (0, 1):
            cells = (
                cell_base[:, None, None]
                + (row_low[:, :, None] + corner_row) * grid_side[:, None, None]
                + col_low[:, None, :]
                + corner_col
            )
            row_part = row_frac if corner_row == 1 else 1.0 - row_frac
            col_part = col_frac if corner_col == 1 else 1.0 - col_frac
            index_list.append(cells.reshape(-1))
            weight_list.append((row_part[:, :, None] * col_part[:, None, :]).reshape(-1))
    return (jnp.stack(index_list), jnp.stack(weight_list))


def head_loss(head_out, roi_table, box_targets, valid_total):
    logits = head_out[:, :CLASSES]
    deltas = head_out[:, CLASSES:]
    labels = roi_table[6]
    valid_f = roi_table[7].astype(jnp.float32)
    onehot = (labels[:, None] == jnp.arange(CLASSES, dtype=jnp.int32)[None, :]).astype(jnp.float32)
    cross_ent = jax.nn.logsumexp(logits, axis=1) - jnp.sum(onehot * logits, axis=1)
    delta_err = deltas - box_targets.T
    absolute = jnp.abs(delta_err)
    huber = jnp.where(absolute < 1.0, 0.5 * delta_err * delta_err, absolute - 0.5)
    foreground = (labels > 0).astype(jnp.float32)
    return jnp.sum(valid_f * (cross_ent + foreground * jnp.sum(huber, axis=1))) / valid_total


def adamw(weight, gradient, moment, square, step_rate):
    new_mean = 0.9 * moment + 0.1 * gradient
    new_square = 0.999 * square + 0.001 * gradient * gradient
    mean_hat = new_mean / (1.0 - 0.9**STEP)
    square_hat = new_square / (1.0 - 0.999**STEP)
    new_weight = weight - step_rate * (mean_hat / (jnp.sqrt(square_hat) + 1e-08) + 0.0001 * weight)
    return (new_weight, new_mean, new_square)


def on_device(
    features,
    roi_table,
    offsets,
    box_targets,
    first_weight,
    first_mean,
    first_square,
    second_weight,
    second_mean,
    second_square,
    out_weight,
    out_mean,
    out_square,
    biases,
    bias_mean,
    bias_square,
):
    roi_count = roi_table.shape[1]
    first_low = first_weight.astype(jnp.bfloat16)
    second_low = second_weight.astype(jnp.bfloat16)
    out_low = out_weight.astype(jnp.bfloat16)
    first_cols, second_cols = (
        lax.all_gather(first_low, "dp", axis=0, tiled=True),
        lax.all_gather(second_low, "dp", axis=0, tiled=True),
    )
    second_full = lax.all_gather(second_cols, "blk", axis=1, tiled=True)
    valid_sum = lax.psum(jnp.sum(roi_table[7].astype(jnp.float32)), ("dp", "blk"))
    valid_total = jnp.maximum(valid_sum, 1.0)
    indices, weights = sample_table(roi_table, offsets)
    pooled_sum = weights[0][:, None] * features[indices[0]].astype(jnp.float32)
    for corner in range(1, 4):
        pooled_sum = pooled_sum + weights[corner][:, None] * features[indices[corner]].astype(
            jnp.float32
        )
    pooled = pooled_sum.reshape(roi_count, K1).astype(jnp.bfloat16)
    first_pre = (
        jnp.dot(
            pooled,
            lax.all_gather(first_cols, "blk", axis=1, tiled=True),
            preferred_element_type=jnp.float32,
        )
        + biases[:H]
    )
    first_act = smooth_unit(first_pre).astype(jnp.bfloat16)
    second_pre = (
        jnp.dot(first_act, second_full, preferred_element_type=jnp.float32) + biases[H : 2 * H]
    )
    second_act = smooth_unit(second_pre).astype(jnp.bfloat16)
    head_out = jnp.dot(second_act, out_low, preferred_element_type=jnp.float32) + biases[2 * H :]

    def local_loss(head_values):
        return head_loss(head_values, roi_table, box_targets, valid_total)

    loss_local, loss_pull = jax.vjp(local_loss, head_out)
    head_grad = loss_pull(jnp.ones_like(loss_local))[0].astype(jnp.bfloat16)
    out_grad = contract_rows(second_act, head_grad)
    second_back = contract_cols(head_grad, out_low)
    second_unit, second_pull = jax.vjp(smooth_unit, second_pre)
    second_grad = second_pull(second_back)[0].astype(jnp.bfloat16)
    first_back = contract_cols(second_grad, second_full)
    first_unit, first_pull = jax.vjp(smooth_unit, first_pre)
    first_grad = first_pull(first_back)[0].astype(jnp.bfloat16)
    bias_grad = jnp.concatenate(
        (
            jnp.sum(first_grad.astype(jnp.float32), axis=0),
            jnp.sum(second_grad.astype(jnp.float32), axis=0),
            jnp.sum(head_grad.astype(jnp.float32), axis=0),
        )
    )
    pooled_grad = contract_cols(first_grad, lax.all_gather(first_cols, "blk", axis=1, tiled=True))
    grad_rows = pooled_grad.reshape(roi_count * 49, C)
    cell_grads = jax.ops.segment_sum(
        weights[0][:, None] * grad_rows, indices[0], num_segments=features.shape[0]
    )
    for corner in range(1, 4):
        cell_grads = cell_grads + jax.ops.segment_sum(
            weights[corner][:, None] * grad_rows, indices[corner], num_segments=features.shape[0]
        )
    cell_grads = cell_grads * third
    feature_grads = lax.psum_scatter(
        cell_grads.astype(jnp.bfloat16), "blk", scatter_dimension=0, tiled=True
    ).astype(jnp.float32)
    out_sum, bias_sum, total_loss = lax.psum((out_grad, bias_grad, loss_local), ("dp", "blk"))
    first_wgrad = contract_rows(pooled, first_grad)
    second_wgrad = contract_rows(first_act, second_grad)
    flat_first, flat_second = (
        lax.psum_scatter(first_wgrad.reshape(-1), "dp", scatter_dimension=0, tiled=True),
        lax.psum_scatter(second_wgrad.reshape(-1), "dp", scatter_dimension=0, tiled=True),
    )
    first_part = flat_first.reshape(-1, H)
    second_part = flat_second.reshape(-1, H)
    first_sum, second_sum = (
        lax.psum_scatter(
            first_part.astype(jnp.bfloat16), "blk", scatter_dimension=1, tiled=True
        ).astype(jnp.float32),
        lax.psum_scatter(
            second_part.astype(jnp.bfloat16), "blk", scatter_dimension=1, tiled=True
        ).astype(jnp.float32),
    )
    first_new, first_mean_new, first_square_new = adamw(
        first_weight, first_sum, first_mean, first_square, rate_first
    )
    second_new, second_mean_new, second_square_new = adamw(
        second_weight, second_sum, second_mean, second_square, rate_second
    )
    out_new, out_mean_new, out_square_new = adamw(
        out_weight, out_sum, out_mean, out_square, rate_out
    )
    bias_new, bias_mean_new, bias_square_new = adamw(
        biases, bias_sum, bias_mean, bias_square, rate_bias
    )
    return (
        feature_grads,
        total_loss,
        first_new,
        first_mean_new,
        first_square_new,
        second_new,
        second_mean_new,
        second_square_new,
        out_new,
        out_mean_new,
        out_square_new,
        bias_new,
        bias_mean_new,
        bias_square_new,
    )


def solution(mesh):
    in_specs = (
        P("dp", None),
        P(None, ("dp", "blk")),
        P(None, "dp"),
        P(None, ("dp", "blk")),
        P("dp", "blk"),
        P("dp", "blk"),
        P("dp", "blk"),
        P("dp", "blk"),
        P("dp", "blk"),
        P("dp", "blk"),
        P(),
        P(),
        P(),
        P(),
        P(),
        P(),
    )
    out_specs = (
        P(("dp", "blk"), None),
        P(),
        P("dp", "blk"),
        P("dp", "blk"),
        P("dp", "blk"),
        P("dp", "blk"),
        P("dp", "blk"),
        P("dp", "blk"),
        P(),
        P(),
        P(),
        P(),
        P(),
        P(),
    )
    return jax.shard_map(
        on_device, mesh=mesh, in_specs=in_specs, out_specs=out_specs, check_vma=False
    )
```

profile of v0, /device:TPU:7, one launch (start us, length us, event | category | flops | bytes accessed | tf_op | source)
XLA Modules:
  0.0 3306.9 jit_solution(8099961324460968532)
XLA Ops:
  9.7 101.5 %all-gather.4.cloned.1.call-done = bf16[12544,256]{1,0:T(8,128)(2,1)} async-done(((bf16[1568,256]{1,0:T(8,128)(2,1)}), bf16[12544,256]{1,0:T(8,128)(2,1)}) %all-gather.4.cloned.1.call-update) | async-done | bytes 6422544 | tf_op jit(solution)/shard_map/all_gather | solution.py:128
  112.2 26.4 all_gather.15
  144.6 35.1 %gather_fusion.3 = bf16[12544,256]{1,0:T(8,128)(2,1)} fusion(bf16[21760,256]{1,0:T(8,128)(2,1)} %param.16, s32[13312]{0:T(1024)S(1)} %pad_clamp_fusion), kind=kCustom, calls=%fused_computation.3 | custom fusion | bytes 12895232 | tf_op jit(solution)/shard_map/gather | solution.py:137
  192.7 14.3 copy.68
  207.0 34.6 %gather_fusion.2 = bf16[12544,256]{1,0:T(8,128)(2,1)} fusion(bf16[21760,256]{1,0:T(8,128)(2,1)} %param.16, s32[13312]{0:T(1024)S(1)} %pad_clamp_fusion.1), kind=kCustom, calls=%fused_computation.2 | custom fusion | bytes 12895232 | tf_op jit(solution)/shard_map/gather | solution.py:137
  254.6 14.2 copy.66
  270.3 34.9 %gather_fusion.1 = bf16[12544,256]{1,0:T(8,128)(2,1)} fusion(bf16[21760,256]{1,0:T(8,128)(2,1)} %param.16, s32[13312]{0:T(1024)S(1)} %pad_clamp_fusion.2), kind=kCustom, calls=%fused_computation.1 | custom fusion | bytes 12895232 | tf_op jit(solution)/shard_map/gather | solution.py:137
  332.3 35.1 %gather_fusion = bf16[12544,256]{1,0:T(8,128)(2,1)} fusion(bf16[21760,256]{1,0:T(8,128)(2,1)} %param.16, s32[13312]{0:T(1024)S(1)} %pad_clamp_fusion.3), kind=kCustom, calls=%fused_computation | custom fusion | bytes 12895232 | tf_op jit(solution)/shard_map/gather | solution.py:135
  400.8 45.4 %psum.28 = f32[]{:T(128)} all-reduce(f32[]{:T(128)} %fusion.53), channel_id=1, replica_groups=mesh['dp'=8,'blk'=4] {'dp','blk'}, use_global_device_ids=true, to_apply=%region_3.0 | all-reduce | flops 1 | bytes 8 | tf_op jit(solution)/shard_map/psum | solution.py:132
  448.1 18.9 fusion.1
  467.1 16.6 multiply_convert_fusion.2
  501.3 22.7 convolution_bitcast_fusion
  524.0 41.8 %copy.69 = f32[1568,8,8,128]{3,1,2,0:T(8,128)} copy(f32[1568,8,8,128]{3,2,1,0:T(8,128)} %convolution_bitcast_fusion) | data formatting | bytes 102760448
  571.2 2116.6 %all-reduce.10 = (bf16[12845056]{0:T(1024)(128)(2,1)}, bf16[1048576]{0:T(1024)(128)(2,1)}) all-reduce(f32[12845056]{0:T(1024)} %bitcast.73, f32[1048576]{0:T(1024)} %bitcast.74), channel_id=3, replica_groups=mesh['dp'=8,'blk'=4] {'dp'}, use_global_device_ids=true, to_apply=%region_15.16.clone | all-reduce | flops 13893632 | bytes 83361792
  2702.3 17.1 fusion.63
  2719.4 14.3 reshape.1021
  2733.7 105.7 %scatter_custom_fusion = f32[21760,256]{1,0:T(8,128)} fusion(s32[12544]{0:T(1024)S(1)} %reshape.1062, f32[12544,256]{1,0:T(8,128)} %reshape.1021, f32[]{:T(128)} %constant.60.clone.1, f32[12544]{0:T(1024)S(1)} %mul.550), kind=kCustom, calls=%fused_computation.24 | custom fusion | flops 6422528 | bytes 35180548 | tf_op jit(solution)/shard_map/scatter-add | solution.py:177
  2839.4 106.0 %scatter_custom_fusion.1 = f32[21760,256]{1,0:T(8,128)} fusion(s32[12544]{0:T(1024)} %get-tuple-element.19, f32[12544,256]{1,0:T(8,128)} %reshape.1021, f32[]{:T(128)} %constant.60.clone.1, f32[12544]{0:T(1024)S(1)} %mul.601), kind=kCustom, calls=%fused_computation.22 | custom fusion | flops 6422528 | bytes 35177984 | tf_op jit(solution)/shard_map/scatter-add | solution.py:181
  2945.4 22.8 add.497
  2968.2 105.7 %scatter_custom_fusion.3 = f32[21760,256]{1,0:T(8,128)} fusion(s32[12544]{0:T(1024)} %get-tuple-element.16, f32[12544,256]{1,0:T(8,128)} %reshape.1021, f32[]{:T(128)} %constant.60.clone.1, f32[12544]{0:T(1024)S(1)} %mul.607), kind=kCustom, calls=%fused_computation.18 | custom fusion | flops 6422528 | bytes 35177984 | tf_op jit(solution)/shard_map/scatter-add | solution.py:181
  3073.9 111.7 %scatter_custom_fusion.2 = f32[21760,256]{1,0:T(8,128)} fusion(f32[21760,256]{1,0:T(8,128)} %add.497, s32[12544]{0:T(1024)S(1)} %reshape.1078, f32[12544,256]{1,0:T(8,128)} %reshape.1021, f32[12544]{0:T(1024)S(1)} %mul.604), kind=kCustom, calls=%fused_computation.20 | custom fusion | flops 6422528 | bytes 35180544 | tf_op jit(solution)/shard_map/scatter-add | solution.py:181
  3185.6 19.0 multiply_convert_fusion
  3205.6 39.7 %all-reduce.4 = (f32[]{:T(128)}, f32[2133]{0:T(1024)S(1)}) all-reduce(f32[]{:T(128)S(6)} %div.117, f32[2133]{0:T(1024)S(1)} %pad_maximum_fusion), channel_id=1, replica_groups=mesh['dp'=8,'blk'=4] {'dp','blk'}, use_global_device_ids=true, to_apply=%region_14.15 | all-reduce | flops 2134 | bytes 17072 | tf_op jit(solution)/shard_map/psum | solution.py:188
  3254.9 40.3 %reduce-scatter.4.cloned.1.call-done = bf16[5440,256]{1,0:T(8,128)(2,1)} async-done(((bf16[21760,256]{1,0:T(8,128)(2,1)}), bf16[5440,256]{1,0:T(8,128)(2,1)}) %reduce-scatter.4.cloned.1.call-update) | async-done | bytes 2785296 | tf_op jit(solution)/shard_map/reduce_scatter | solution.py:185
  (138 shorter events, 148.7 us)
Async XLA Ops:
  7.2 104.0 %all-gather.4.cloned.1.call-start = ((), (), s32[]{:S(2)}) async-start(), calls=%async_computation.3 | async-start | bytes 7225344 | tf_op jit(solution)/shard_map/all_gather | solution.py:128
  9.6 457.5 %all-gather.6.cloned.1.call-start = ((), (), s32[]{:S(2)}) async-start(), calls=%async_computation.4 | async-start | bytes 32112640 | tf_op jit(solution)/shard_map/all_gather | solution.py:144
  111.2 372.5 %all-gather.8.cloned.1.call-start = ((), (), s32[]{:S(2)}) async-start(), calls=%async_computation.5 | async-start | bytes 2621440 | tf_op jit(solution)/shard_map/all_gather | solution.py:131
  138.7 3107.2 %all-reduce.9.cloned.1.call-start = ((), (), s32[]{:S(2)}) async-start(), calls=%async_computation.9 | async-start | bytes 720896 | tf_op jit(solution)/shard_map/psum | solution.py:188
  143.1 36.6 %copy-start = (s32[256,7,7]{2,1,0:T(8,128)}, s32[256,7,7]{2,1,0:T(8,128)S(1)}, u32[]{:S(2)}) copy-start(s32[256,7,7]{2,1,0:T(8,128)S(1)} %get-tuple-element.52) | copy-start | bytes 150532
  143.1 125.7 %copy-start.2 = (s32[256,7,7]{2,1,0:T(8,128)}, s32[256,7,7]{2,1,0:T(8,128)S(1)}, u32[]{:S(2)}) copy-start(s32[256,7,7]{2,1,0:T(8,128)S(1)} %get-tuple-element.53) | copy-start | bytes 150532
  380.4 66.5 %copy-start.20 = (u32[32]{0:T(128)S(1)}, u32[32]{0:T(128)}, u32[]{:S(2)}) copy-start(u32[32]{0:T(128)} %constant.53) | copy-start | bytes 388
  398.1 69.0 %copy-start.4 = (f32[256,7,7]{2,1,0:T(8,128)}, f32[256,7,7]{2,1,0:T(8,128)S(1)}, u32[]{:S(2)}) copy-start(f32[256,7,7]{2,1,0:T(8,128)S(1)} %get-tuple-element.51) | copy-start | bytes 150532
  398.1 69.0 %copy-start.5 = (f32[256,7,7]{2,1,0:T(8,128)}, f32[256,7,7]{2,1,0:T(8,128)S(1)}, u32[]{:S(2)}) copy-start(f32[256,7,7]{2,1,0:T(8,128)S(1)} %get-tuple-element.49) | copy-start | bytes 150532
  501.3 22.7 copy-start.9
  571.1 2118.6 %copy-start.3 = (s32[256,7,7]{2,1,0:T(8,128)S(1)}, s32[256,7,7]{2,1,0:T(8,128)}, u32[]{:S(2)}) copy-start(s32[256,7,7]{2,1,0:T(8,128)} %copy-done.2) | copy-start | bytes 150532
  571.1 2122.6 %copy-start.1 = (s32[256,7,7]{2,1,0:T(8,128)S(1)}, s32[256,7,7]{2,1,0:T(8,128)}, u32[]{:S(2)}) copy-start(s32[256,7,7]{2,1,0:T(8,128)} %copy-done) | copy-start | bytes 150532
  571.1 2677.2 %reduce-scatter.8.cloned.1.call-start = ((), (), s32[]{:S(2)}) async-start(), calls=%async_computation.8 | async-start | bytes 327680 | tf_op jit(solution)/shard_map/reduce_scatter | solution.py:201
  2689.7 560.4 %reduce-scatter.6.cloned.1.call-start = ((), (), s32[]{:S(2)}) async-start(), calls=%async_computation.7 | async-start | bytes 4014080 | tf_op jit(solution)/shard_map/reduce_scatter | solution.py:198
  2702.3 592.9 %reduce-scatter.4.cloned.1.call-start = ((), (), s32[]{:S(2)}) async-start(), calls=%async_computation.6 | async-start | bytes 13926400 | tf_op jit(solution)/shard_map/reduce_scatter | solution.py:185
  3185.6 19.1 copy-start.18
  3185.6 19.1 copy-start.19
  3185.6 59.6 %copy-start.13 = (f32[2133]{0:T(1024)S(1)}, f32[2133]{0:T(1024)}, u32[]{:S(2)}) copy-start(f32[2133]{0:T(1024)} %param.29) | copy-start | bytes 25600
  3185.6 59.6 %copy-start.14 = (f32[2133]{0:T(1024)S(1)}, f32[2133]{0:T(1024)}, u32[]{:S(2)}) copy-start(f32[2133]{0:T(1024)} %param.30) | copy-start | bytes 25600
  3185.6 59.6 %copy-start.15 = (f32[2133]{0:T(1024)S(1)}, f32[2133]{0:T(1024)}, u32[]{:S(2)}) copy-start(f32[2133]{0:T(1024)} %param.31) | copy-start | bytes 25600
  3204.7 43.7 %copy-start.10 = (f32[128,256]{1,0:T(8,128)S(1)}, f32[128,256]{1,0:T(8,128)}, u32[]{:S(2)}) copy-start(f32[128,256]{1,0:T(8,128)} %param.23) | copy-start | bytes 393220
  3204.7 43.7 %copy-start.11 = (f32[128,256]{1,0:T(8,128)S(1)}, f32[128,256]{1,0:T(8,128)}, u32[]{:S(2)}) copy-start(f32[128,256]{1,0:T(8,128)} %param.24) | copy-start | bytes 393220
  3204.7 45.4 %copy-start.6 = (f32[1568,256]{1,0:T(8,128)S(1)}, f32[1568,256]{1,0:T(8,128)}, u32[]{:S(2)}) copy-start(f32[1568,256]{1,0:T(8,128)} %param.20) | copy-start | bytes 4816900
  3204.7 45.4 %copy-start.7 = (f32[1568,256]{1,0:T(8,128)S(1)}, f32[1568,256]{1,0:T(8,128)}, u32[]{:S(2)}) copy-start(f32[1568,256]{1,0:T(8,128)} %param.21) | copy-start | bytes 4816900
  (5 other events, 55.0 us)
Sparse Core Ops, SparseCore 0:
  10.8 100.4 all-gather.3
  112.8 160.2 all-gather.5
  274.6 22.8 all-gather.7
  571.2 170.8 all-reduce.8
  2689.8 20.1 reduce-scatter.7
  2713.0 38.3 reduce-scatter.5
  3204.8 90.2 reduce-scatter.3
where the time goes:
time: 3320 us; the launch traced here: 3310 us
  blocking collectives  2230 us (67%)
  other arithmetic  516 us (16%)
  local copies, waits for them, and re-layouts  330 us (10%)
  waiting for transfers between devices  142 us (4%)
  matrix products  72.5 us (2%)
    unnamed x1, blocking collectives  2120 us
    scatter-add x3, other arithmetic, on_device(): jax.ops.segment_sum(weights[corner][:, None] * grad_rows, indices[corner]...  323 us
    scatter-add x1, other arithmetic, on_device(): jax.ops.segment_sum(weights[0][:, None] * grad_rows, indices[0], num_segm...  106 us
    gather x3, local copies, waits for them, and re-layouts, on_device(): features[indices[corner]].astype(jnp.float32)  105 us
    all_gather x1, waiting for transfers between devices, on_device(): lax.all_gather(first_low, 'dp', axis=0, tiled=True)  102 us
    convert_element_type x6, local copies, waits for them, and re-layouts, on_device(): features[indices[corner]].astype(jnp.float32)  81.6 us
  transfers between devices with their start and end apart: 7, of which 2 were waited for; matrix products, arithmetic and copies ran while one was open for 25% of the time, Pallas kernels for 0%

commit v1 on v0

v1 whole, which is shorter than its diff:
```python
import functools

import jax
import jax.numpy as jnp
import numpy as np
from jax import lax
from jax.experimental import pallas as pl
from jax.experimental.pallas import tpu as pltpu
from jax.sharding import PartitionSpec as P

C = 256
H = 1024
CLASSES = 81
CANVAS = 512
IMAGES = 4
LEVELS = 4
STEP = 10
K1 = 12544
BINS = 49

HALF = 128
SLOTS = 26
KQ = SLOTS * HALF
FAR = -1.0e6
BATCH = 16
LANES = 512
SIDES = (128, 64, 32, 16)
BASES = (0, 16384, 20480, 21504)
WIN_ROWS = (52, 28, 16, 16)
WIN_COLS = (64, 32, 16, 16)
BACK_COLS = (56, 32, 16, 16)
VMEM_LIMIT = 60 * 1024 * 1024
GROUP = 32
OWNED = 13
SHARD = OWNED + 1
AHEAD = H // 2
SWAPPED = 9
LATER = OWNED - SWAPPED
AHEAD_ROWS = (OWNED + 2) * GROUP
MESH = pl.DeviceIdType.MESH

third = 1.0 / 3.0
rate_first = 0.018
rate_second = 0.06
rate_out = 0.18
rate_bias = 0.2


def contract_rows(left_side, right_side):
    return lax.dot_general(
        left_side, right_side, (((0,), (0,)), ((), ())), preferred_element_type=jnp.float32
    )


def contract_cols(left_side, right_side):
    return lax.dot_general(
        left_side, right_side, (((1,), (1,)), ((), ())), preferred_element_type=jnp.float32
    )


def sort_rois(roi_table, box_targets):
    count = roi_table.shape[1]
    key = roi_table[5] * IMAGES + roi_table[4]
    place = jnp.arange(count, dtype=jnp.int32)
    before = (key[None, :] < key[:, None]) | (
        (key[None, :] == key[:, None]) & (place[None, :] < place[:, None])
    )
    rank = jnp.sum(before.astype(jnp.int32), axis=1)
    segments = jnp.arange(LEVELS * IMAGES + 1, dtype=jnp.int32)
    starts = jnp.sum((key[None, :] < segments[:, None]).astype(jnp.int32), axis=1)
    rows = jnp.concatenate((roi_table.astype(jnp.float32), box_targets), axis=0)
    pick = (rank[None, :] == place[:, None]).astype(jnp.float32)
    ordered = lax.dot_general(
        pick, rows, (((1,), (1,)), ((), ())), precision=lax.Precision.HIGHEST
    )
    return ordered[:, :8].astype(jnp.int32).T, ordered[:, 8:], starts


def sample_points(table, offsets, parity):
    level_of = table[5]
    image_of = table[4]
    choose = (image_of[:, None] == jnp.arange(IMAGES, dtype=jnp.int32)[None, :]).astype(jnp.int32)
    shift_y = jnp.sum(choose * offsets[0][None, :], axis=1)
    shift_x = jnp.sum(choose * offsets[1][None, :], axis=1)
    grid_side = jnp.right_shift(jnp.full_like(level_of, CANVAS // 4), level_of)
    stride_px = (4 * jnp.left_shift(jnp.ones_like(level_of), level_of)).astype(jnp.float32)
    bins = 2 * jnp.arange(SLOTS, dtype=jnp.int32) + parity
    inside = bins < BINS
    every = jnp.arange(7, dtype=jnp.int32)

    def axis_points(low_edge, high_edge, shift_by, which, keep):
        centres = (which.astype(jnp.float32) + 0.5) / 7.0
        start_px = (low_edge + shift_by).astype(jnp.float32)
        extent = (high_edge - low_edge).astype(jnp.float32)
        points = start_px[:, None] + centres[None, :] * extent[:, None]
        limit_max = (grid_side - 1).astype(jnp.float32)[:, None]
        scaled = jnp.clip(points / stride_px[:, None] - 0.5, 0.0, limit_max)
        return jnp.where(keep[None, :], scaled, FAR)

    rows = (table[1], table[3], shift_y)
    cols = (table[0], table[2], shift_x)
    return (
        axis_points(*rows, every, every >= 0),
        axis_points(*cols, every, every >= 0),
        axis_points(*rows, bins // 7, inside),
        axis_points(*cols, bins % 7, inside),
    )


def window_lows(offsets):
    lows = []
    for level in range(LEVELS - 1):
        half_stride = 2 << level
        lows.append(jnp.maximum(jnp.right_shift(offsets - half_stride, 2 + level), 0))
    lows.append(jnp.zeros_like(offsets))
    return jnp.stack(lows, axis=1).reshape(-1)


def segment_loop(starts, lows, visit):
    for level in range(LEVELS):

        def image_step(image, carry, level=level):
            segment = level * IMAGES + image
            begin = starts[segment]
            end = starts[segment + 1]
            row_low = lows[level * IMAGES + image]
            col_low = lows[(LEVELS + level) * IMAGES + image]

            @pl.when(end > begin)
            def _():
                visit(level, begin, end, row_low, col_low)

            return carry

        lax.fori_loop(0, IMAGES, image_step, 0)


def hat(distance):
    return jnp.maximum(1.0 - jnp.abs(distance), 0.0)


def pool_kernel(starts, lows, meta, feat_hbm, uv_ref, out_ref, raw, cells, win, acc, sem):
    total = raw.shape[0]
    lane0 = pl.multiple_of(meta[0] * HALF, HALF)
    fetch = pltpu.make_async_copy(feat_hbm.at[:, pl.ds(lane0, HALF)], raw, sem)
    fetch.start()
    count = acc.shape[0]

    def clear(step, carry):
        acc[pl.ds(pl.multiple_of(step * 8, 8), 8), :] = jnp.zeros((8, KQ), jnp.float32)
        return carry

    lax.fori_loop(0, count // 8, clear, 0)
    fetch.wait()

    def widen(step, carry):
        rows = pl.ds(pl.multiple_of(step * 128, 128), 128)
        cells[rows, :] = raw[rows, :].astype(jnp.float32)
        return carry

    lax.fori_loop(0, total // 128, widen, 0)

    def visit(level, begin, end, row_low, col_low):
        side, base = SIDES[level], BASES[level]
        height, width = WIN_ROWS[level], WIN_COLS[level]
        shift = width.bit_length() - 1
        per_tile = HALF // width
        tiles = height // per_tile
        depth = tiles * HALF

        def take(row, carry):
            source = pl.ds(base + (row_low + row) * side + col_low, width)
            target = pl.ds(pl.multiple_of(row * width, width), width)
            win[target, :] = cells[source, :].astype(jnp.bfloat16)
            return carry

        lax.fori_loop(0, height, take, 0)
        row_shift = row_low.astype(jnp.float32)
        col_shift = col_low.astype(jnp.float32)

        def group(parity, step, carry):
            first = pl.multiple_of(step * BATCH, BATCH)
            lane = lax.broadcasted_iota(jnp.int32, (BATCH, HALF), 1)
            lane_row = jnp.right_shift(lane, shift).astype(jnp.float32) + row_shift
            lane_col = jnp.bitwise_and(lane, width - 1).astype(jnp.float32) + col_shift
            roi = first + lax.broadcasted_iota(jnp.int32, (BATCH, HALF), 0)
            mine = (roi >= begin) & (roi < end)
            points = jnp.where(mine, uv_ref[pl.ds(first, BATCH), :], FAR)
            row_at = [points[:, a : a + 1] - lane_row for a in range(7)]
            col_hats = [hat(points[:, 64 + b : 65 + b] - lane_col) for b in range(7)]
            bins = [2 * slot + parity for slot in range(SLOTS)]
            pooled = None
            for begin_tile in range(0, tiles, 4):
                columns = []
                for tile in range(begin_tile, min(begin_tile + 4, tiles)):
                    row_hats = [hat(at - float(tile * per_tile)) for at in row_at]
                    weights = [
                        (row_hats[one // 7] * col_hats[one % 7]).astype(jnp.bfloat16)
                        if one < BINS
                        else jnp.zeros((BATCH, HALF), jnp.bfloat16)
                        for one in bins
                    ]
                    columns.append(jnp.concatenate(weights, axis=0))
                part = jnp.dot(
                    jnp.concatenate(columns, axis=1),
                    win[begin_tile * HALF : (begin_tile + len(columns)) * HALF, :],
                    preferred_element_type=jnp.float32,
                )
                pooled = part if pooled is None else pooled + part
            for slot in range(SLOTS):
                where = (pl.ds(first, BATCH), slice(slot * HALF, (slot + 1) * HALF))
                acc[where] = acc[where] + pooled[slot * BATCH : (slot + 1) * BATCH, :]
            return carry

        for parity in (0, 1):

            @pl.when(meta[1] == parity)
            def _(parity=parity):
                lax.fori_loop(
                    begin // BATCH, (end + BATCH - 1) // BATCH, functools.partial(group, parity), 0
                )

    segment_loop(starts, lows, visit)

    def narrow(step, carry):
        rows = pl.ds(pl.multiple_of(step * 16, 16), 16)
        out_ref[rows, :] = acc[rows, :].astype(jnp.bfloat16)
        return carry

    lax.fori_loop(0, count // 16, narrow, 0)


def pool(features, meta, starts, lows, points):
    count = points.shape[0]
    cells = features.shape[0]
    return pl.pallas_call(
        pool_kernel,
        out_shape=jax.ShapeDtypeStruct((count, KQ), jnp.bfloat16),
        in_specs=[
            pl.BlockSpec(memory_space=pltpu.SMEM),
            pl.BlockSpec(memory_space=pltpu.SMEM),
            pl.BlockSpec(memory_space=pltpu.SMEM),
            pl.BlockSpec(memory_space=pl.ANY),
            pl.BlockSpec(memory_space=pltpu.VMEM),
        ],
        out_specs=pl.BlockSpec(memory_space=pltpu.VMEM),
        scratch_shapes=[
            pltpu.VMEM((cells, HALF), jnp.bfloat16),
            pltpu.VMEM((cells, HALF), jnp.float32),
            pltpu.VMEM((KQ, HALF), jnp.bfloat16),
            pltpu.VMEM((count, KQ), jnp.float32),
            pltpu.SemaphoreType.DMA,
        ],
        compiler_params=pltpu.CompilerParams(vmem_limit_bytes=VMEM_LIMIT),
        cost_estimate=pl.CostEstimate(
            flops=40_000_000_000, bytes_accessed=13_000_000, transcendentals=0
        ),
        name="pool_bins",
    )(starts, lows, meta, features, points)


def spread_kernel(
    starts,
    lows,
    grad_ref,
    weight_hbm,
    row_ref,
    col_ref,
    out_ref,
    weight_ref,
    pooled,
    cells,
    part,
    row_hat,
    right,
    weight_sem,
):
    total = cells.shape[0]
    fetch = pltpu.make_async_copy(weight_hbm, weight_ref, weight_sem)
    fetch.start()

    def clear(step, carry):
        rows = pl.ds(pl.multiple_of(step * 128, 128), 128)
        cells[rows, :] = jnp.zeros((128, HALF), jnp.float32)
        return carry

    lax.fori_loop(0, total // 128, clear, 0)
    fetch.wait()

    def back_dot(step, carry):
        cols = pl.ds(pl.multiple_of(step * 256, 256), 256)
        pooled[:, cols] = contract_cols(grad_ref[...], weight_ref[cols, :]).astype(jnp.bfloat16)
        return carry

    lax.fori_loop(0, KQ // 256, back_dot, 0)
    right[SLOTS * BATCH :, :] = jnp.zeros((LANES - SLOTS * BATCH, HALF), jnp.bfloat16)

    def visit(level, begin, end, row_low, col_low):
        side, base = SIDES[level], BASES[level]
        height, width = WIN_ROWS[level], BACK_COLS[level]
        chunk = (26, 28, 16, 16)[level]
        row_shift = row_low.astype(jnp.float32)
        col_shift = col_low.astype(jnp.float32)

        def wipe(row, carry):
            rows = pl.ds(pl.multiple_of(row * width, 8), width)
            part[rows, :] = jnp.zeros((width, HALF), jnp.float32)
            return carry

        lax.fori_loop(0, height, wipe, 0)

        def group(step, carry):
            first = pl.multiple_of(step * BATCH, BATCH)
            for slot in range(SLOTS):
                right[slot * BATCH : (slot + 1) * BATCH, :] = pooled[
                    pl.ds(first, BATCH), slot * HALF : (slot + 1) * HALF
                ]
            lane = lax.broadcasted_iota(jnp.int32, (1, LANES), 1)
            roi = first + jnp.bitwise_and(lane, BATCH - 1)
            mine = (roi >= begin) & (roi < end)
            row_at = jnp.where(mine, row_ref[pl.ds(step, 1), :], FAR) - row_shift
            col_at = jnp.where(mine, col_ref[pl.ds(step, 1), :], FAR) - col_shift
            row_hat[...] = hat(
                row_at - lax.broadcasted_iota(jnp.int32, (56, LANES), 0).astype(jnp.float32)
            )
            col_hat = hat(
                col_at - lax.broadcasted_iota(jnp.int32, (width, LANES), 0).astype(jnp.float32)
            )
            for row in range(0, height, chunk):
                left = jnp.concatenate(
                    [col_hat * row_hat[row + one : row + one + 1, :] for one in range(chunk)], axis=0
                ).astype(jnp.bfloat16)
                rows = slice(row * width, (row + chunk) * width)
                part[rows, :] += jnp.dot(left, right[...], preferred_element_type=jnp.float32)
            return carry

        lax.fori_loop(begin // BATCH, (end + BATCH - 1) // BATCH, group, 0)

        def flush(row, carry):
            target = pl.ds(base + (row_low + row) * side + col_low, width)
            source = pl.ds(pl.multiple_of(row * width, 8), width)
            cells[target, :] = cells[target, :] + part[source, :]
            return carry

        lax.fori_loop(0, height, flush, 0)

    segment_loop(starts, lows, visit)

    def narrow(step, carry):
        rows = pl.ds(pl.multiple_of(step * 128, 128), 128)
        out_ref[rows, :] = (cells[rows, :] * third).astype(jnp.bfloat16)
        return carry

    lax.fori_loop(0, total // 128, narrow, 0)


def spread(first_grad, weight, starts, lows, rows_at, cols_at, cells):
    count = first_grad.shape[0]
    return pl.pallas_call(
        spread_kernel,
        out_shape=jax.ShapeDtypeStruct((cells, HALF), jnp.bfloat16),
        in_specs=[
            pl.BlockSpec(memory_space=pltpu.SMEM),
            pl.BlockSpec(memory_space=pltpu.SMEM),
            pl.BlockSpec(memory_space=pltpu.VMEM),
            pl.BlockSpec(memory_space=pl.ANY),
            pl.BlockSpec(memory_space=pltpu.VMEM),
            pl.BlockSpec(memory_space=pltpu.VMEM),
        ],
        out_specs=pl.BlockSpec(memory_space=pltpu.VMEM),
        scratch_shapes=[
            pltpu.VMEM((KQ, H), jnp.bfloat16),
            pltpu.VMEM((count, KQ), jnp.bfloat16),
            pltpu.VMEM((cells, HALF), jnp.float32),
            pltpu.VMEM((WIN_ROWS[0] * BACK_COLS[0], HALF), jnp.float32),
            pltpu.VMEM((56, LANES), jnp.float32),
            pltpu.VMEM((LANES, HALF), jnp.bfloat16),
            pltpu.SemaphoreType.DMA,
        ],
        compiler_params=pltpu.CompilerParams(vmem_limit_bytes=VMEM_LIMIT),
        cost_estimate=pl.CostEstimate(
            flops=40_000_000_000, bytes_accessed=15_000_000, transcendentals=0
        ),
        name="spread_bins",
    )(starts, lows, first_grad, weight, rows_at, cols_at)


def adamw(weight, gradient, moment, square, step_rate):
    new_mean = 0.9 * moment + 0.1 * gradient
    new_square = 0.999 * square + 0.001 * gradient * gradient
    mean_hat = new_mean / (1.0 - 0.9**STEP)
    square_hat = new_square / (1.0 - 0.999**STEP)
    new_weight = weight - step_rate * (mean_hat / (jnp.sqrt(square_hat) + 1e-08) + 0.0001 * weight)
    return (new_weight, new_mean, new_square)


def groups_before(half, parity, index):
    inside = index % 16 - (8 * parity + 4 * half)
    return index // 16 * 4 + jnp.minimum(jnp.maximum(inside, 0), 4)


def group_place(half, parity, slot, part, n_dp):
    span = K1 // GROUP // n_dp

    def earlier(index):
        inside = jnp.bitwise_and(index, 15) - (8 * parity + 4 * half)
        return jnp.right_shift(index, 4) * 4 + jnp.minimum(jnp.maximum(inside, 0), 4)

    group = 8 * (2 * slot + parity) + 4 * half + part
    owner = sum((group >= span * other).astype(jnp.int32) for other in range(1, n_dp))
    return owner, earlier(group) - earlier(owner * span)


def owned_groups(n_dp):
    span = K1 // GROUP // n_dp
    table = np.zeros((n_dp, 4, OWNED), np.int32)
    for owner in range(n_dp):
        for quarter in range(4):
            found = [
                local
                for local in range(span)
                if (owner * span + local) // 8 % 2 == quarter % 2
                and (owner * span + local) % 8 // 4 == quarter // 2
            ]
            table[owner, quarter] = (found + [0] * OWNED)[:OWNED]
    return table


def group_sources(n_dp):
    span = K1 // GROUP // n_dp
    table = np.zeros((n_dp, span), np.int32)
    for owner in range(n_dp):
        met = [0] * 4
        for local in range(span):
            group = owner * span + local
            quarter = group % 8 // 4 * 2 + group // 8 % 2
            table[owner, local] = quarter * OWNED + met[quarter]
            met[quarter] += 1
    return table


def by_groups(n_dp):
    return n_dp == 8


def deal_kernel(table, weight_ref, rois_ref, out_ref):
    base = lax.axis_index("dp") * 4 * OWNED
    for quarter in range(4):

        def step(index, carry, quarter=quarter):
            source = pl.ds(
                pl.multiple_of(table[base + quarter * OWNED + index] * GROUP, GROUP), GROUP
            )
            target = pl.ds(pl.multiple_of(index * GROUP, GROUP), GROUP)
            out_ref[quarter, target, :] = weight_ref[source, :].astype(jnp.bfloat16)
            return carry

        lax.fori_loop(0, OWNED, step, 0)
        out_ref[quarter, OWNED * GROUP :, :] = rois_ref[...]


def gather_quarter(first_weight, second_weight, rois, n_dp):
    cols = first_weight.shape[1]
    second = second_weight.astype(jnp.bfloat16)
    if by_groups(n_dp):
        table = jnp.asarray(owned_groups(n_dp).reshape(-1))
        top = lax.optimization_barrier(rois[8:].astype(jnp.bfloat16))
        rest = rois[8:] - top.astype(jnp.float32)
        middle_term = lax.optimization_barrier(rest.astype(jnp.bfloat16))
        last = (rest - middle_term.astype(jnp.float32)).astype(jnp.bfloat16)
        riders = jnp.concatenate((rois[:8].astype(jnp.bfloat16), top, middle_term, last), axis=0)
        riders = jnp.pad(riders, ((0, GROUP - riders.shape[0]), (0, 0)))
        dealt = pl.pallas_call(
            deal_kernel,
            out_shape=jax.ShapeDtypeStruct((4, SHARD * GROUP, cols), jnp.bfloat16),
            in_specs=[
                pl.BlockSpec(memory_space=pltpu.SMEM),
                pl.BlockSpec(memory_space=pltpu.VMEM),
                pl.BlockSpec(memory_space=pltpu.VMEM),
            ],
            out_specs=pl.BlockSpec(memory_space=pltpu.VMEM),
            name="deal_rows",
        )(table, first_weight, riders)
        swapped = lax.all_to_all(dealt, "blk", split_axis=0, concat_axis=0, tiled=True)
        ridden = swapped[:, OWNED * GROUP :].astype(jnp.float32).transpose(1, 0, 2)
        ridden = ridden.reshape(GROUP, -1)
        all_rois = jnp.concatenate(
            (ridden[:8], (ridden[8:12] + ridden[12:16]) + ridden[16:20]), axis=0
        )
        rows = swapped[:, : OWNED * GROUP].transpose(1, 0, 2).reshape(OWNED * GROUP, -1)
        block = second.reshape(2, 2, GROUP, cols).transpose(0, 2, 1, 3).reshape(2 * GROUP, -1)
        ahead = jnp.concatenate((rows[:, :AHEAD], block), axis=0)
        gathered = lax.all_gather(ahead, "dp", axis=0, tiled=True)
        behind = rows[:, AHEAD:]
        swapped = lax.ppermute(behind, "dp", [(spot, spot ^ 1) for spot in range(n_dp)])
        return (gathered, behind, swapped), all_rois
    all_rois = lax.all_gather(rois, "blk", axis=1, tiled=True)
    rows = lax.all_gather(first_weight.astype(jnp.bfloat16), "dp", axis=0, tiled=True)
    split = jnp.pad(rows.reshape(BINS, C, cols), ((0, 2 * SLOTS - BINS), (0, 0), (0, 0)))
    split = split.reshape(SLOTS, 2, 2, HALF, cols).transpose(2, 1, 0, 3, 4)
    split = split.reshape(4, KQ, cols)
    mine = lax.all_to_all(split, "blk", split_axis=0, concat_axis=0, tiled=True)
    mine = mine.transpose(1, 0, 2).reshape(KQ, -1)
    second = lax.all_gather(second, "dp", axis=0, tiled=True)
    block = second.reshape(4, -1, cols).transpose(1, 0, 2).reshape(-1, 4 * cols)
    rows = jnp.concatenate((mine, block), axis=0)
    return (rows, rows, rows), all_rois


def second_blocks(source, target, column, sem, n_dp):
    owners, rows = (n_dp, GROUP) if by_groups(n_dp) else (1, H // 4)
    copies = []
    for owner in range(owners):
        for part in range(4):
            if by_groups(n_dp):
                first = owner * AHEAD_ROWS + (OWNED + part // 2) * GROUP
                lane = part % 2 * 256
            else:
                first, lane = KQ, part * 256
            copies.append(
                pltpu.make_async_copy(
                    source.at[pl.ds(first, rows), pl.ds(lane, 256)],
                    target.at[pl.ds((owner * 4 + part) * rows, rows), column],
                    sem.at[owner * 4 + part],
                )
            )
    return copies


def owner_rows(half, parity, owner, n_dp):
    span = K1 // GROUP // n_dp
    begin = groups_before(half, parity, owner * span)
    end = groups_before(half, parity, (owner + 1) * span)
    many = pl.ds(pl.multiple_of(begin * GROUP, GROUP), (OWNED - 1) * GROUP)
    last = pl.ds(pl.multiple_of((end - 1) * GROUP, GROUP), GROUP)
    return many, last, end - begin == OWNED


def ahead_copies(source, target, sems, half, parity, n_dp):
    copies = []
    for owner in range(n_dp):
        many, last, full = owner_rows(half, parity, owner, n_dp)
        first, rows = owner * AHEAD_ROWS, (OWNED - 1) * GROUP
        copies.append(
            (
                None,
                pltpu.make_async_copy(
                    source.at[pl.ds(first, rows), :], target.at[many, :], sems.at[2 * owner]
                ),
            )
        )
        copies.append(
            (
                full,
                pltpu.make_async_copy(
                    source.at[pl.ds(first + rows, GROUP), :],
                    target.at[last, :],
                    sems.at[2 * owner + 1],
                ),
            )
        )
    return copies


def whole_copies(source, targets, sems):
    return [
        (
            None,
            pltpu.make_async_copy(
                source.at[pl.ds(0, KQ), pl.ds(half * AHEAD, AHEAD)], target, sems.at[half]
            ),
        )
        for half, target in enumerate(targets)
    ]


def each_copy(copies, action):
    for condition, copy in copies:
        if condition is None:
            action(copy)
        else:

            @pl.when(condition)
            def _(copy=copy):
                action(copy)


def wipe_slots(target, parity):
    target[KQ - HALF :, :] = jnp.zeros((HALF, AHEAD), jnp.bfloat16)

    @pl.when(parity == 1)
    def _():
        target[KQ - 2 * HALF : KQ - HALF, :] = jnp.zeros((HALF, AHEAD), jnp.bfloat16)


def gelu_parts(values):
    cdf = 0.5 * (1.0 + lax.erf(values * np.float32(np.sqrt(0.5))))
    density = jnp.exp(-0.5 * values * values) * np.float32(1.0 / np.sqrt(2.0 * np.pi))
    return values * cdf, cdf + values * density


def middle_kernel(
    n_dp,
    pooled_hbm,
    ahead_hbm,
    behind_hbm,
    swapped_hbm,
    predict_ref,
    bias_ref,
    aux_ref,
    valid_ref,
    all_grad,
    second_out,
    tail_ref,
    ordered_hbm,
    pooled,
    ahead,
    behind,
    second_ref,
    part,
    sent,
    came,
    first_pre,
    second_pre,
    first_act,
    second_act,
    first_grad,
    second_grad,
    valid_came,
    pooled_sem,
    weight_sem,
    own_sem,
    second_sem,
    out_sem,
    up_send,
    up_recv,
    down_send,
    down_recv,
    y_send,
    y_recv,
    valid_send,
    valid_recv,
    send_sem,
    recv_sem,
):
    me = lax.axis_index("blk")
    dp = lax.axis_index("dp")
    peers = [(dp + step) % n_dp for step in range(1, n_dp)] if by_groups(n_dp) else []
    high, low = me // 2, me % 2
    sibling = high * 2 + (1 - low)
    across = (1 - high) * 2 + low
    corner = (1 - high) * 2 + (1 - low)
    rows = part.shape[0]
    quarter = H // 4

    barrier = pltpu.get_barrier_semaphore()
    for other in (sibling, across, corner):
        pl.semaphore_signal(barrier, inc=1, device_id={"blk": other}, device_id_type=MESH)
    for peer in peers:
        pl.semaphore_signal(barrier, inc=1, device_id={"dp": peer}, device_id_type=MESH)

    def hidden_cols(which):
        return pl.ds(pl.multiple_of(which * quarter, quarter), quarter)

    z, y = dp // 2, dp % 2
    partner = 2 * z + 1 - y
    shard = (OWNED - 1) * GROUP

    def shard_pieces(owner):
        many, last, full = owner_rows(high, low, owner, n_dp)
        first = many.start
        return (
            (None, pl.ds(pl.multiple_of(first, GROUP), shard // 2), pl.ds(0, shard // 2)),
            (
                None,
                pl.ds(pl.multiple_of(first + shard // 2, GROUP), shard // 2),
                pl.ds(shard // 2, shard // 2),
            ),
            (full, last, pl.ds(shard, GROUP)),
        )

    def shard_copies(owner, send, recv, index, target, own=False):
        copies = []
        for piece, (condition, place, source) in enumerate(shard_pieces(owner)):
            copies.append(
                (
                    condition,
                    pltpu.make_async_remote_copy(
                        src_ref=behind_hbm.at[source, :] if own else behind.at[place, :],
                        dst_ref=behind.at[place, :],
                        send_sem=send.at[3 * index + piece],
                        recv_sem=recv.at[3 * index + piece],
                        device_id={"dp": target},
                        device_id_type=MESH,
                    ),
                )
            )
        return copies

    def own_shard(action):
        @pl.when(z < 3)
        def _():
            each_copy(shard_copies(dp, up_send, up_recv, 0, dp + 2, True), action)

        @pl.when(z > 0)
        def _():
            each_copy(shard_copies(dp, down_send, down_recv, 0, dp - 2, True), action)

    def relay_shards(distance, took, action):
        def pass_on(owner, send, recv, neighbour, goes_on, place):
            coming = shard_copies(owner, send, recv, distance - 1, neighbour)
            aside = shard_copies(owner, y_send, y_recv, place, partner)
            onward = [None] * len(coming)
            if distance < 3:
                onward = shard_copies(owner, send, recv, distance, neighbour)
            for came_in, on, over in zip(coming, onward, aside):
                each_copy([came_in], took)
                if on is not None:

                    @pl.when(goes_on)
                    def _(on=on):
                        each_copy([on], action)

                each_copy([over], action)

        @pl.when(z >= distance)
        def _():
            pass_on(dp - 2 * distance, up_send, up_recv, dp + 2, z < 3, z - distance)

        @pl.when(z + distance <= 3)
        def _():
            pass_on(dp + 2 * distance, down_send, down_recv, dp - 2, z > 0, z + distance)

    def serve(distance):
        if by_groups(n_dp):
            relay_shards(distance, lambda copy: copy.wait_recv(), lambda copy: copy.start())

    blocks = second_blocks(ahead_hbm, second_ref, hidden_cols(me), second_sem, n_dp)
    for copy in blocks:
        copy.start()
    if by_groups(n_dp):
        early = ahead_copies(ahead_hbm, ahead, weight_sem, high, low, n_dp)
        late = []
        for which, (source_hbm, owner) in enumerate(((behind_hbm, dp), (swapped_hbm, partner))):
            for piece, (condition, place, source) in enumerate(shard_pieces(owner)):
                late.append(
                    (
                        condition,
                        pltpu.make_async_copy(
                            source_hbm.at[source, :],
                            behind.at[place, :],
                            out_sem.at[2 + 3 * which + piece],
                        ),
                    )
                )
        wipe_slots(ahead, low)
        wipe_slots(behind, low)
    else:
        early, late = whole_copies(ahead_hbm, (ahead, behind), weight_sem), []
    each_copy((*early, *late), lambda copy: copy.start())

    def chunk_rows(which):
        return pl.ds(pl.multiple_of(which * rows, 16), rows)

    order = (corner, across, sibling, me)
    chunks = [
        pltpu.make_async_copy(
            pooled_hbm.at[chunk_rows(which), :], pooled.at[chunk_rows(which), :], pooled_sem.at[i]
        )
        for i, which in enumerate(order)
    ]
    for chunk in chunks:
        chunk.start()
    pl.semaphore_wait(barrier, 3 + len(peers))
    counts = [
        pltpu.make_async_remote_copy(
            src_ref=valid_ref,
            dst_ref=valid_came.at[index],
            send_sem=valid_send.at[index],
            recv_sem=valid_recv.at[index],
            device_id={"dp": peer},
            device_id_type=MESH,
        )
        for index, peer in enumerate(peers)
    ]
    if by_groups(n_dp):
        own_shard(lambda copy: copy.start())
    for copy in counts:
        copy.start()

    def remote(source, target, index, other):
        return pltpu.make_async_remote_copy(
            src_ref=source,
            dst_ref=target,
            send_sem=send_sem.at[index],
            recv_sem=recv_sem.at[index],
            device_id={"blk": other},
            device_id_type=MESH,
        )

    for copy in blocks:
        copy.wait()
    mine, theirs = second_ref.at[:, hidden_cols(me)], second_ref.at[:, hidden_cols(across)]
    second_sibling = remote(mine, mine, 3, sibling)
    second_across = remote(mine, mine, 4, across)
    second_forward = remote(theirs, theirs, 5, sibling)
    second_across.start()
    second_sibling.start()

    def in_blocks(count, body):
        def step(index, carry):
            body(index)
            return carry

        lax.fori_loop(0, count, step, 0)

    def block32(step):
        return pl.ds(pl.multiple_of(step * 32, 32), 32)

    def first_half_product(which):
        cols = slice(which * AHEAD, (which + 1) * AHEAD)
        weight = (ahead, behind)[which]
        base = 18 * which
        to_sibling = remote(sent.at[0, :, cols], came.at[0, :, cols], base, sibling)
        to_across = remote(sent.at[1, :, cols], came.at[1, :, cols], base + 1, across)
        to_sibling_last = remote(sent.at[2, :, cols], came.at[2, :, cols], base + 2, sibling)

        def chunk_dot(i):
            if which == 0:
                chunks[i].wait()

            def cols_dot(step):
                lanes = pl.ds(pl.multiple_of(step * 256, 256), 256)
                target = pl.ds(pl.multiple_of(which * AHEAD + step * 256, 256), 256)
                part[:, target] = jnp.dot(
                    pooled[chunk_rows(order[i]), :],
                    weight[:, lanes],
                    preferred_element_type=jnp.float32,
                )

            in_blocks(AHEAD // 256, cols_dot)

        def hand_on(slot, came_slot=None):
            def store(step):
                block = block32(step)
                value = part[block, cols]
                if came_slot is not None:
                    value = value + came[came_slot, block, cols].astype(jnp.float32)
                sent[slot, block, cols] = value.astype(jnp.bfloat16)

            in_blocks(rows // 32, store)

        def step0():
            chunk_dot(0)
            hand_on(0)
            to_sibling.start()

        def step1():
            chunk_dot(1)
            to_sibling.wait_recv()
            hand_on(1, 0)
            to_across.start()

        def step2():
            chunk_dot(2)
            hand_on(2)
            to_sibling_last.start()

        def step3():
            chunk_dot(3)
            to_sibling_last.wait_recv()
            to_across.wait_recv()

            def activate(step):
                block = block32(step)
                value = (
                    part[block, cols]
                    + came[1, block, cols].astype(jnp.float32)
                    + came[2, block, cols].astype(jnp.float32)
                    + bias_ref[0:1, cols]
                )
                first_pre[block, cols] = value
                first_act[block, cols] = gelu_parts(value)[0].astype(jnp.bfloat16)

            in_blocks(rows // 32, activate)

        return (step0, step1, step2, step3), (to_sibling, to_across, to_sibling_last)

    steps, sums = first_half_product(0)
    each_copy(early, lambda copy: copy.wait())
    steps[0]()
    steps[1]()
    serve(1)
    second_across.wait_recv()
    second_forward.start()
    steps[2]()
    serve(2)
    steps[3]()
    serve(3)
    each_copy(late, lambda copy: copy.wait())
    if by_groups(n_dp):
        for place in range(4):

            @pl.when(z != place)
            def _(place=place):
                each_copy(
                    shard_copies(2 * place + 1 - y, y_send, y_recv, place, partner),
                    lambda copy: copy.wait_recv(),
                )
    ordered_copies = [
        pltpu.make_async_copy(
            source, ordered_hbm.at[:, pl.ds(which * AHEAD, AHEAD)], out_sem.at[which]
        )
        for which, source in enumerate((ahead, behind))
    ]
    for copy in ordered_copies:
        copy.start()
    steps, more_sums = first_half_product(1)
    for step in steps:
        step()
    my_rows = chunk_rows(me)
    across_rows = chunk_rows(across)
    second_sibling.wait_recv()
    second_forward.wait_recv()

    def second_dot(step):
        cols = pl.ds(pl.multiple_of(step * 256, 256), 256)
        second_pre[:, cols] = (
            jnp.dot(first_act[...], second_ref[:, cols], preferred_element_type=jnp.float32)
            + bias_ref[1:2, cols]
        )

    in_blocks(H // 256, second_dot)

    def activate_second(step):
        block = block32(step)
        second_act[block, :] = gelu_parts(second_pre[block, :])[0].astype(jnp.bfloat16)

    in_blocks(rows // 32, activate_second)
    head_out = (
        jnp.dot(second_act[...], predict_ref[...], preferred_element_type=jnp.float32)
        + bias_ref[2:3, :HALF]
    )
    lane = lax.broadcasted_iota(jnp.int32, (rows, HALF), 1)
    is_logit = lane < CLASSES
    is_delta = (lane >= CLASSES) & (lane < CLASSES + 4)
    label = aux_ref[:, 0:1]
    valid_total = valid_ref[0:1, 0:1]
    for index, copy in enumerate(counts):
        copy.wait_recv()
        valid_total = valid_total + valid_came[index, 0:1, 0:1]
    share = aux_ref[:, 1:2] / jnp.maximum(valid_total, 1.0)
    foreground = (label > 0.5).astype(jnp.float32)
    onehot = (lane.astype(jnp.float32) == label).astype(jnp.float32)
    top = jnp.max(jnp.where(is_logit, head_out, -jnp.inf), axis=1, keepdims=True)
    exped = jnp.where(is_logit, jnp.exp(jnp.minimum(head_out - top, 0.0)), 0.0)
    exp_sum = jnp.sum(exped, axis=1, keepdims=True)
    chosen = jnp.sum(onehot * head_out, axis=1, keepdims=True)
    error = jnp.where(is_delta, head_out - aux_ref[...], 0.0)
    absolute = jnp.abs(error)
    huber = jnp.where(absolute < 1.0, 0.5 * error * error, absolute - 0.5)
    huber_sum = jnp.sum(jnp.where(is_delta, huber, 0.0), axis=1, keepdims=True)
    loss_rows = share * (jnp.log(exp_sum) + top - chosen + foreground * huber_sum)
    delta_slope = foreground * jnp.minimum(jnp.maximum(error, -1.0), 1.0)
    head_grad = (share * (exped / exp_sum - jnp.where(is_logit, onehot, 0.0) + delta_slope)).astype(
        jnp.bfloat16
    )
    wide = head_grad.astype(jnp.float32)
    lane1 = lax.broadcasted_iota(jnp.int32, (1, HALF), 1)
    head_bias = jnp.sum(wide, axis=0, keepdims=True) + jnp.where(
        lane1 == CLASSES + 4, jnp.sum(loss_rows, axis=0, keepdims=True), 0.0
    )

    def second_back(step):
        cols = pl.ds(pl.multiple_of(step * 256, 256), 256)
        back = contract_cols(head_grad, predict_ref[cols, :])
        second_grad[:, cols] = (back * gelu_parts(second_pre[:, cols])[1]).astype(jnp.bfloat16)

    in_blocks(H // 256, second_back)
    def first_back(step):
        cols = slice(step * quarter, (step + 1) * quarter)
        back = contract_cols(second_grad[...], second_ref[cols, :])
        first_grad[:, cols] = (back * gelu_parts(first_pre[:, cols])[1]).astype(jnp.bfloat16)
        source, target = first_grad.at[:, cols], all_grad.at[my_rows, cols]
        to_other = remote(source, target, 6 + step, across)
        to_twin = remote(source, target, 10 + step, sibling)
        to_other.start()
        to_twin.start()
        relayed = all_grad.at[across_rows, cols]
        return to_other, to_twin, remote(relayed, relayed, 14 + step, sibling)

    grad_copies = [first_back(step) for step in range(4)]
    grad_own = pltpu.make_async_copy(first_grad, all_grad.at[my_rows, :], own_sem.at[2])
    grad_own.start()

    def bias_rows(grads):
        total = jnp.sum(grads[...].astype(jnp.float32), axis=0, keepdims=True)
        return [total[:, i * HALF : (i + 1) * HALF] for i in range(H // HALF)]

    nothing = jnp.zeros((1, HALF), jnp.float32)
    bias_sums = (
        bias_rows(first_grad),
        bias_rows(second_grad),
        [head_bias] + [nothing] * 7,
        [nothing] * 8,
    )
    for step in range(4):
        piece = contract_rows(second_act[:, step * quarter : (step + 1) * quarter], head_grad)
        if by_groups(n_dp):
            for owner in range(n_dp):
                tail_ref[step, owner, :32, :] = piece[owner * 32 : owner * 32 + 32, :]
                tail_ref[step, owner, 32:, :] = jnp.concatenate(
                    [bias_sums[step][owner]] + [nothing] * 7, axis=0
                )
        else:
            tail_ref[step, :quarter, :] = piece
            tail_ref[step, quarter:, :] = jnp.concatenate(bias_sums[step], axis=0)

    for to_other, _, relay in grad_copies:
        to_other.wait_recv()
        relay.start()

    def second_block(step):
        cols = pl.ds(pl.multiple_of(step * 256, 256), 256)
        second_out[:, cols] = contract_rows(first_act[...], second_grad[:, cols]).astype(
            jnp.bfloat16
        )

    in_blocks(H // 256, second_block)
    grad_own.wait()
    for _, to_twin, relay in grad_copies:
        to_twin.wait_recv()
        relay.wait_recv()
    for copy in ordered_copies:
        copy.wait()
    if by_groups(n_dp):

        def sent_off(copy):
            copy.wait_send()

        own_shard(sent_off)
        for distance in (1, 2, 3):
            relay_shards(distance, lambda copy: None, sent_off)
    for copy in (
        *sums,
        *more_sums,
        second_sibling,
        second_across,
        second_forward,
        *(copy for three in grad_copies for copy in three),
        *counts,
    ):
        copy.wait_send()


def middle(pooled, ahead, behind, swapped, predict, bias, aux, valid_here, n_dp):
    count = pooled.shape[0]
    rows = aux.shape[0]
    tail = (4, n_dp, 40, HALF) if by_groups(n_dp) else (4, H // 4 + 8, HALF)
    any_spec = pl.BlockSpec(memory_space=pl.ANY)
    vmem_spec = pl.BlockSpec(memory_space=pltpu.VMEM)
    return pl.pallas_call(
        functools.partial(middle_kernel, n_dp),
        out_shape=(
            jax.ShapeDtypeStruct((count, H), jnp.bfloat16),
            jax.ShapeDtypeStruct((H, H), jnp.bfloat16),
            jax.ShapeDtypeStruct(tail, jnp.float32),
            jax.ShapeDtypeStruct((KQ, H), jnp.bfloat16),
        ),
        in_specs=[any_spec] * 4 + [vmem_spec] * 4,
        out_specs=(any_spec, vmem_spec, vmem_spec, any_spec),
        scratch_shapes=[
            pltpu.VMEM((count, KQ), jnp.bfloat16),
            pltpu.VMEM((KQ, AHEAD), jnp.bfloat16),
            pltpu.VMEM((KQ, AHEAD), jnp.bfloat16),
            pltpu.VMEM((H, H), jnp.bfloat16),
            pltpu.VMEM((rows, H), jnp.float32),
            pltpu.VMEM((3, rows, H), jnp.bfloat16),
            pltpu.VMEM((3, rows, H), jnp.bfloat16),
            pltpu.VMEM((rows, H), jnp.float32),
            pltpu.VMEM((rows, H), jnp.float32),
            pltpu.VMEM((rows, H), jnp.bfloat16),
            pltpu.VMEM((rows, H), jnp.bfloat16),
            pltpu.VMEM((rows, H), jnp.bfloat16),
            pltpu.VMEM((rows, H), jnp.bfloat16),
            pltpu.VMEM((7, 8, HALF), jnp.float32),
            pltpu.SemaphoreType.DMA((4,)),
            pltpu.SemaphoreType.DMA((SLOTS,)),
            pltpu.SemaphoreType.DMA((3,)),
            pltpu.SemaphoreType.DMA((4 * n_dp if by_groups(n_dp) else 4,)),
            pltpu.SemaphoreType.DMA((8,)),
            pltpu.SemaphoreType.DMA((9,)),
            pltpu.SemaphoreType.DMA((9,)),
            pltpu.SemaphoreType.DMA((9,)),
            pltpu.SemaphoreType.DMA((9,)),
            pltpu.SemaphoreType.DMA((12,)),
            pltpu.SemaphoreType.DMA((12,)),
            pltpu.SemaphoreType.DMA((7,)),
            pltpu.SemaphoreType.DMA((7,)),
            pltpu.SemaphoreType.DMA((21,)),
            pltpu.SemaphoreType.DMA((21,)),
        ],
        compiler_params=pltpu.CompilerParams(
            vmem_limit_bytes=VMEM_LIMIT, collective_id=0, has_side_effects=True
        ),
        cost_estimate=pl.CostEstimate(
            flops=9_000_000_000, bytes_accessed=25_000_000, transcendentals=1_500_000
        ),
        name="middle",
    )(pooled, ahead, behind, swapped, predict, bias, aux, valid_here)


def weight_grad_kernel(n_dp, meta, pooled_ref, grad_ref, here_hbm, there_hbm, later_hbm, stage, sems):
    half, parity, y = meta[0], meta[1], meta[2]
    step = pl.program_id(0)
    last = pl.num_programs(0) - 1

    def copies(which):
        buffer = which % 2
        for one in range(256 // GROUP):
            slot = 2 * which + one // 4
            owner, local = group_place(half, parity, slot, one % 4, n_dp)
            row = jnp.right_shift(owner, 1)
            inside = slot < SLOTS - 1 - parity
            here = jnp.bitwise_and(owner, 1) == y
            there = jnp.logical_not(here)
            for condition, target, place in (
                (here, here_hbm, row * OWNED + local),
                (there & (local < SWAPPED), there_hbm, row * SWAPPED + local),
                (there & (local >= SWAPPED), later_hbm, row * LATER + local - SWAPPED),
            ):

                @pl.when(inside & condition)
                def _(target=target, one=one, place=place):
                    rows = pl.ds(pl.multiple_of(place * GROUP, GROUP), GROUP)
                    pltpu.make_async_copy(
                        stage.at[buffer, pl.ds(one * GROUP, GROUP), :],
                        target.at[rows, :],
                        sems.at[buffer, one],
                    ).start()

    def waits(which):
        buffer = which % 2
        for one in range(256 // GROUP):

            @pl.when(2 * which + one // 4 < SLOTS - 1 - parity)
            def _(one=one):
                rows = pl.ds(one * GROUP, GROUP)
                pltpu.make_async_copy(
                    stage.at[buffer, rows, :], here_hbm.at[rows, :], sems.at[buffer, one]
                ).wait()

    @pl.when(step >= 2)
    def _():
        waits(step - 2)

    stage[step % 2] = contract_rows(pooled_ref[...], grad_ref[...]).astype(jnp.bfloat16)
    copies(step)

    @pl.when(step == last)
    def _():
        waits(step - 1)
        waits(step)


def weight_grad(pooled, all_grad, meta, n_dp):
    count = pooled.shape[0]
    shapes = tuple(
        jax.ShapeDtypeStruct((n_dp // 2 * groups * GROUP, H), jnp.bfloat16)
        for groups in (OWNED, SWAPPED, LATER)
    )
    any_spec = pl.BlockSpec(memory_space=pl.ANY)
    return pl.pallas_call(
        functools.partial(weight_grad_kernel, n_dp),
        grid=(SLOTS // 2,),
        out_shape=shapes,
        in_specs=[
            pl.BlockSpec(memory_space=pltpu.SMEM),
            pl.BlockSpec((count, 256), lambda i: (0, i)),
            pl.BlockSpec((count, H), lambda i: (0, 0)),
        ],
        out_specs=(any_spec, any_spec, any_spec),
        scratch_shapes=[
            pltpu.VMEM((2, 256, H), jnp.bfloat16),
            pltpu.SemaphoreType.DMA((2, 256 // GROUP)),
        ],
        compiler_params=pltpu.CompilerParams(vmem_limit_bytes=VMEM_LIMIT),
        cost_estimate=pl.CostEstimate(
            flops=7_000_000_000, bytes_accessed=16_000_000, transcendentals=0
        ),
        name="weight_grad",
    )(meta, pooled, all_grad)


def reduce_kernel(
    n_dp,
    here_hbm,
    swapped_hbm,
    later_hbm,
    tail_ref,
    second_ref,
    cells_hbm,
    home_ref,
    second_out,
    tails_ref,
    kept_hbm,
    far_hbm,
    cells_kept,
    cells_near,
    cells_own,
    cells_sum,
    mine,
    y_came,
    up_came,
    down_came,
    final,
    tail_near,
    tail_mine,
    tail_came,
    second_came,
    tail_send,
    tail_recv,
    second_send,
    second_recv,
    cells_load,
    cells_send,
    cells_recv,
    shard_load,
    y_send,
    y_recv,
    up_send,
    up_recv,
    down_send,
    down_recv,
    home_send,
    home_recv,
):
    dp = lax.axis_index("dp")
    me = lax.axis_index("blk")
    half, parity = me // 2, me % 2
    z, y = dp // 2, dp % 2
    home_rows = OWNED * GROUP
    quarter = H // 4
    sibling, across = me // 2 * 2 + 1 - me % 2, (me + 2) % 4
    others = ((me + 1) % 4, (me + 2) % 4, (me + 3) % 4)
    has_below, has_above = z > 0, z < 3

    barrier = pltpu.get_barrier_semaphore()

    def greet(**where):
        pl.semaphore_signal(barrier, inc=1, device_id=where, device_id_type=MESH)

    peers = tuple((dp + step) % n_dp for step in range(1, n_dp))
    for peer in peers:
        greet(dp=peer)
    for other in others:
        greet(blk=other)

    def order(k):
        near, far = ((3, 3), (2, 0), (1, 2), (0, 1))[k]
        low_side = jnp.where(z % 3 == 0, near, far)
        return jnp.where(z < 2, low_side, 3 - low_side)

    def shard_loads(k):
        target = order(k)
        rows = pl.ds(pl.multiple_of(target * home_rows, GROUP), home_rows)
        some = SWAPPED * GROUP
        swapped = pl.ds(pl.multiple_of(target * some, GROUP), some)
        return [
            pltpu.make_async_copy(here_hbm.at[rows, :], mine.at[target], shard_load.at[2 * k]),
            pltpu.make_async_copy(
                swapped_hbm.at[swapped, :],
                y_came.at[target, pl.ds(0, some)],
                shard_load.at[2 * k + 1],
            ),
        ]

    for k in range(4):
        for copy in shard_loads(k):
            copy.start()
    pl.semaphore_wait(barrier, n_dp + 2)

    def remote(source, target, send, recv, **where):
        return pltpu.make_async_remote_copy(
            src_ref=source,
            dst_ref=target,
            send_sem=send,
            recv_sem=recv,
            device_id=where,
            device_id_type=MESH,
        )

    piece = tail_ref.shape[2]
    nears, seconds = [], []
    for index, other in enumerate(others):
        nears.append(
            remote(
                tail_ref.at[other],
                tail_near.at[index],
                tail_send.at[index],
                tail_recv.at[index],
                blk=other,
            )
        )
        seconds.append(
            remote(
                second_ref.at[:, pl.ds(pl.multiple_of(other * quarter, quarter), quarter)],
                second_came.at[index],
                second_send.at[index],
                second_recv.at[index],
                blk=other,
            )
        )

    quarter_cells = cells_sum.shape[0]

    def cell_rows(which):
        return cells_hbm.at[pl.ds(pl.multiple_of(which * quarter_cells, 16), quarter_cells), :]

    loads, gives = [], []
    for index, chip in enumerate((1 - half, half)):
        loads.append(
            pltpu.make_async_copy(
                cell_rows(2 * chip + parity), cells_own.at[index], cells_load.at[index]
            )
        )
        gives.append(
            remote(
                cell_rows(2 * chip + 1 - parity),
                cells_near.at[index],
                cells_send.at[index],
                cells_recv.at[index],
                blk=sibling,
            )
        )
    kept_out = pltpu.make_async_copy(cells_kept, kept_hbm, cells_load.at[2])
    crossing = remote(cells_sum, far_hbm, cells_send.at[2], cells_recv.at[2], blk=across)
    parts = (pl.ds(0, SWAPPED * GROUP), pl.ds(SWAPPED * GROUP, LATER * GROUP))

    def y_copy(k):
        target = order(k)
        rows = pl.ds(pl.multiple_of(target * LATER * GROUP, GROUP), LATER * GROUP)
        return remote(
            later_hbm.at[rows, :],
            y_came.at[target, parts[1]],
            y_send.at[k],
            y_recv.at[k],
            dp=2 * z + 1 - y,
        )

    for k in range(4):
        y_copy(k).start()
    for copy in (*nears, *seconds, *gives, *loads):
        copy.start()

    def cell_blocks(body):
        def step(index, carry):
            body(pl.ds(pl.multiple_of(index * 160, 160), 160))
            return carry

        lax.fori_loop(0, quarter_cells // 160, step, 0)

    def give_across():
        loads[0].wait()
        gives[0].wait_recv()

        def add(rows):
            cells_sum[rows, :] = (
                cells_own[0, rows, :].astype(jnp.float32)
                + cells_near[0, rows, :].astype(jnp.float32)
            ).astype(jnp.bfloat16)

        cell_blocks(add)
        crossing.start()

    def keep_here():
        loads[1].wait()
        gives[1].wait_recv()

        def add(rows):
            cells_kept[rows, :] = cells_own[1, rows, :].astype(jnp.float32) + cells_near[
                1, rows, :
            ].astype(jnp.float32)

        cell_blocks(add)
        kept_out.start()

    def add_up(target, sources, part):
        first, groups = ((0, SWAPPED), (SWAPPED, LATER))[part]

        def step(index, carry):
            rows = pl.ds(pl.multiple_of((first + index) * GROUP, GROUP), GROUP)
            total = mine[target, rows, :].astype(jnp.float32)
            for ref in sources:
                total = total + ref[target, rows, :].astype(jnp.float32)
            mine[target, rows, :] = total.astype(jnp.bfloat16)
            return carry

        lax.fori_loop(0, groups, step, 0)

    def z_copy(target, part, came, send, recv, neighbour):
        sem = 2 * target + part
        return remote(
            mine.at[target, parts[part]],
            came.at[target, parts[part]],
            send.at[sem],
            recv.at[sem],
            dp=neighbour,
        )

    def up_copy(target, part):
        return z_copy(target, part, up_came, up_send, up_recv, dp + 2)

    def down_copy(target, part):
        return z_copy(target, part, down_came, down_send, down_recv, dp - 2)

    def arrive(k, part):
        if part == 0:
            for copy in shard_loads(k):
                copy.wait()
        else:
            y_copy(k).wait_recv()

    def chain(k, part):
        target = order(k)
        arrive(k, part)

        @pl.when(target > z)
        def _():
            @pl.when(has_below)
            def _():
                up_copy(target, part).wait_recv()
                add_up(target, (y_came, up_came), part)

            @pl.when(jnp.logical_not(has_below))
            def _():
                add_up(target, (y_came,), part)

            up_copy(target, part).start()

        @pl.when(target < z)
        def _():
            @pl.when(has_above)
            def _():
                down_copy(target, part).wait_recv()
                add_up(target, (y_came, down_came), part)

            @pl.when(jnp.logical_not(has_above))
            def _():
                add_up(target, (y_came,), part)

            down_copy(target, part).start()

    def last(part):
        arrive(3, part)
        add_up(z, (y_came,), part)

        @pl.when(has_below)
        def _():
            up_copy(z, part).wait_recv()
            add_up(z, (up_came,), part)

        @pl.when(has_above)
        def _():
            down_copy(z, part).wait_recv()
            add_up(z, (down_came,), part)

    def home_copies(part):
        copies = []
        for index, other in enumerate(others):
            cols = pl.ds(pl.multiple_of(other * quarter, quarter), quarter)
            copies.append(
                remote(
                    mine.at[z, parts[part], cols],
                    final.at[me, parts[part]],
                    home_send.at[3 * part + index],
                    home_recv.at[3 * part + index],
                    blk=other,
                )
            )
        return copies

    chain(0, 0)
    give_across()
    for copy in nears:
        copy.wait_recv()
    tail_mine[...] = tail_ref[me] + tail_near[0] + tail_near[1] + tail_near[2]
    tails = []
    for index, peer in enumerate(peers):
        sem = 3 + index
        tails.append(
            remote(
                tail_mine.at[peer],
                tail_came.at[index],
                tail_send.at[sem],
                tail_recv.at[sem],
                dp=peer,
            )
        )
    for copy in tails:
        copy.start()
    chain(1, 0)
    for copy in tails:
        copy.wait_recv()
    my_tail = pl.ds(pl.multiple_of((me * n_dp + dp) * piece, 8), piece)
    total = tail_mine[dp]
    for index in range(n_dp - 1):
        total = total + tail_came[index]
    tails_ref[my_tail, :] = total
    spreads = []
    for index, peer in enumerate(peers):
        spot = tails_ref.at[my_tail, :]
        sem = n_dp + 2 + index
        spreads.append(remote(spot, spot, tail_send.at[sem], tail_recv.at[sem], dp=peer))
    for copy in spreads:
        copy.start()
    keep_here()
    chain(2, 0)
    last(0)
    homes = home_copies(0)
    for copy in homes:
        copy.start()
    for k in range(3):
        chain(k, 1)
    block = tails_ref.at[pl.ds(pl.multiple_of(me * n_dp * piece, 8), n_dp * piece), :]
    shares = []
    for index, other in enumerate(others):
        sem = 2 * n_dp + 1 + index
        shares.append(remote(block, block, tail_send.at[sem], tail_recv.at[sem], blk=other))
    for copy in spreads:
        copy.wait_recv()
    for copy in shares:
        copy.start()
    own_cols = pl.ds(pl.multiple_of(me * quarter, quarter), quarter)
    second = second_ref[:, own_cols].astype(jnp.float32)
    for index, copy in enumerate(seconds):
        copy.wait_recv()
        second = second + second_came[index].astype(jnp.float32)
    second_out[...] = second
    last(1)
    homes_later = home_copies(1)
    for copy in homes_later:
        copy.start()
    home_ref[pl.ds(pl.multiple_of(me * home_rows, GROUP), home_rows), :] = mine[z, :, own_cols]
    for copy in shares:
        copy.wait_recv()
    for index in range(3):
        sender = (me + 3 - index) % 4
        homes[index].wait_recv()
        homes_later[index].wait_recv()
        rows = pl.ds(pl.multiple_of(sender * home_rows, GROUP), home_rows)
        home_ref[rows, :] = final[sender]
    for copy in (
        *homes,
        *homes_later,
        *nears,
        *tails,
        *spreads,
        *shares,
        *seconds,
        *gives,
        crossing,
        *(y_copy(k) for k in range(4)),
    ):
        copy.wait_send()
    kept_out.wait()
    crossing.wait_recv()
    for k in range(3):
        target = order(k)

        @pl.when(target > z)
        def _():
            up_copy(target, 0).wait_send()
            up_copy(target, 1).wait_send()

        @pl.when(target < z)
        def _():
            down_copy(target, 0).wait_send()
            down_copy(target, 1).wait_send()


def reduce_home(here, swapped, later, tail, second, cell_grads, n_dp):
    home = OWNED * GROUP
    piece = tail.shape[2]
    cells = cell_grads.shape[0] // 4
    vmem_spec = pl.BlockSpec(memory_space=pltpu.VMEM)
    any_spec = pl.BlockSpec(memory_space=pl.ANY)
    shards = pltpu.VMEM((4, home, H), jnp.bfloat16)

    def sems(number):
        return pltpu.SemaphoreType.DMA((number,))

    return pl.pallas_call(
        functools.partial(reduce_kernel, n_dp),
        out_shape=(
            jax.ShapeDtypeStruct((4 * home, H // 4), jnp.bfloat16),
            jax.ShapeDtypeStruct((H // n_dp, H // 4), jnp.float32),
            jax.ShapeDtypeStruct((4 * n_dp * piece, HALF), jnp.float32),
            jax.ShapeDtypeStruct((cells, HALF), jnp.float32),
            jax.ShapeDtypeStruct((cells, HALF), jnp.bfloat16),
        ),
        in_specs=[any_spec, any_spec, any_spec, vmem_spec, vmem_spec, any_spec],
        out_specs=(vmem_spec,) * 3 + (any_spec,) * 2,
        scratch_shapes=[
            pltpu.VMEM((cells, HALF), jnp.float32),
            pltpu.VMEM((2, cells, HALF), jnp.bfloat16),
            pltpu.VMEM((2, cells, HALF), jnp.bfloat16),
            pltpu.VMEM((cells, HALF), jnp.bfloat16),
            shards,
            shards,
            shards,
            shards,
            pltpu.VMEM((4, home, H // 4), jnp.bfloat16),
            pltpu.VMEM((3, n_dp, piece, HALF), jnp.float32),
            pltpu.VMEM((n_dp, piece, HALF), jnp.float32),
            pltpu.VMEM((n_dp - 1, piece, HALF), jnp.float32),
            pltpu.VMEM((3, H // n_dp, H // 4), jnp.bfloat16),
            sems(2 * n_dp + 4),
            sems(2 * n_dp + 4),
            sems(3),
            sems(3),
            sems(3),
            sems(3),
            sems(3),
            sems(8),
            sems(4),
            sems(4),
            sems(8),
            sems(8),
            sems(8),
            sems(8),
            sems(6),
            sems(6),
        ],
        compiler_params=pltpu.CompilerParams(
            vmem_limit_bytes=VMEM_LIMIT, collective_id=1, has_side_effects=True
        ),
        cost_estimate=pl.CostEstimate(
            flops=60_000_000_000, bytes_accessed=200_000_000, transcendentals=0
        ),
        name="reduce_home",
    )(here, swapped, later, tail, second, cell_grads)


def sum_apart(pooled, all_grad, n_blk):
    first_wgrad = contract_rows(pooled, all_grad).astype(jnp.bfloat16)
    split = first_wgrad.reshape(KQ, n_blk, -1).transpose(1, 0, 2)
    mine = lax.all_to_all(split, "blk", split_axis=0, concat_axis=0, tiled=True)
    cols = mine.shape[2]
    mine = mine.reshape(2, 2, SLOTS, HALF, cols).transpose(2, 1, 0, 3, 4)
    mine = mine.reshape(2 * SLOTS, C, cols)[:BINS].reshape(K1, cols)
    first_sum = lax.psum_scatter(mine, "dp", scatter_dimension=0, tiled=True).astype(jnp.float32)
    return first_sum


def finish_kernel(
    table,
    home_ref,
    weight_ref,
    mean_ref,
    square_ref,
    kept_ref,
    far_ref,
    new_ref,
    new_mean_ref,
    new_square_ref,
    features_ref,
):
    groups = weight_ref.shape[0] // GROUP
    span = K1 // GROUP // lax.axis_size("dp")
    base = lax.axis_index("dp") * span + pl.program_id(0) * groups
    my_half = lax.axis_index("blk") // 2
    for index in range(groups):
        source = pl.ds(pl.multiple_of(table[base + index] * GROUP, GROUP), GROUP)
        rows = slice(index * GROUP, (index + 1) * GROUP)
        updated = adamw(
            weight_ref[rows, :],
            home_ref[source, :].astype(jnp.float32),
            mean_ref[rows, :],
            square_ref[rows, :],
            rate_first,
        )
        new_ref[rows, :], new_mean_ref[rows, :], new_square_ref[rows, :] = updated
    for half in range(2):

        @pl.when(my_half == half)
        def _(half=half):
            features_ref[:, half * HALF : (half + 1) * HALF] = kept_ref[...]
            features_ref[:, (1 - half) * HALF : (2 - half) * HALF] = far_ref[...].astype(
                jnp.float32
            )


def finish(home, kept, far, first_weight, first_mean, first_square, n_dp):
    cols = first_weight.shape[1]
    steps = 7
    table = jnp.asarray(group_sources(n_dp).reshape(-1))
    block = pl.BlockSpec((first_weight.shape[0] // steps, cols), lambda i: (i, 0))
    shape = jax.ShapeDtypeStruct(first_weight.shape, jnp.float32)
    cells = kept.shape[0]
    some = -(-cells // steps // 16) * 16
    part = pl.BlockSpec((some, HALF), lambda i: (i, 0))
    return pl.pallas_call(
        finish_kernel,
        grid=(steps,),
        out_shape=(shape, shape, shape, jax.ShapeDtypeStruct((cells, C), jnp.float32)),
        in_specs=[
            pl.BlockSpec(memory_space=pltpu.SMEM),
            pl.BlockSpec(memory_space=pltpu.VMEM),
            block,
            block,
            block,
            part,
            part,
        ],
        out_specs=(block, block, block, pl.BlockSpec((some, C), lambda i: (i, 0))),
        compiler_params=pltpu.CompilerParams(vmem_limit_bytes=VMEM_LIMIT),
        name="finish",
    )(table, home, first_weight, first_mean, first_square, kept, far)


def on_device(
    features,
    roi_table,
    offsets,
    box_targets,
    first_weight,
    first_mean,
    first_square,
    second_weight,
    second_mean,
    second_square,
    out_weight,
    out_mean,
    out_square,
    biases,
    bias_mean,
    bias_square,
    n_dp,
    n_blk,
):
    place = lax.axis_index("blk")
    half = place // 2
    parity = place % 2
    roi_count = roi_table.shape[1]
    outw = out_weight.shape[1]
    rois = jnp.concatenate((roi_table.astype(jnp.float32), box_targets), axis=0)
    weight, all_rois = gather_quarter(first_weight, second_weight, rois, n_dp)
    valid_here = jnp.broadcast_to(jnp.sum(all_rois[7]), (8, HALF))
    if not by_groups(n_dp):
        valid_here = lax.psum(valid_here, "dp")
    predict = jnp.pad(out_weight.astype(jnp.bfloat16), ((0, 0), (0, HALF - outw)))
    bias = jnp.zeros((8, H), jnp.float32)
    bias = bias.at[0].set(biases[:H]).at[1].set(biases[H : 2 * H]).at[2, :outw].set(biases[2 * H :])

    table, targets, starts = sort_rois(all_rois[:8].astype(jnp.int32), all_rois[8:])
    lows = window_lows(offsets)
    row_sevens, col_sevens, rows_at, cols_at = sample_points(table, offsets, parity)
    apart = ((0, 0), (0, 64 - 7))
    points = jnp.concatenate((jnp.pad(row_sevens, apart), jnp.pad(col_sevens, apart)), axis=1)

    def by_group(values):
        grouped = values.reshape(-1, BATCH, SLOTS).transpose(0, 2, 1).reshape(-1, SLOTS * BATCH)
        return jnp.pad(grouped, ((0, 0), (0, LANES - SLOTS * BATCH)), constant_values=FAR)

    my_table = lax.dynamic_slice_in_dim(table, place * roi_count, roi_count, axis=1)
    my_targets = lax.dynamic_slice_in_dim(targets, place * roi_count, roi_count, axis=0)
    aux = jnp.concatenate(
        (
            my_table[6].astype(jnp.float32)[:, None],
            my_table[7].astype(jnp.float32)[:, None],
            jnp.zeros((roi_count, CLASSES - 2), jnp.float32),
            my_targets,
            jnp.zeros((roi_count, HALF - CLASSES - 4), jnp.float32),
        ),
        axis=1,
    )
    meta = jnp.stack((half, parity, lax.axis_index("dp") % 2))
    pooled = pool(features, meta, starts, lows, points)
    all_grad, second_wgrad, tail, ordered = middle(
        pooled, *weight, predict, bias, aux, valid_here, n_dp
    )
    second_part = lax.psum_scatter(second_wgrad, "dp", scatter_dimension=0, tiled=True)
    if by_groups(n_dp):
        here, there, later = weight_grad(pooled, all_grad, meta, n_dp)
        swapped = lax.ppermute(there, "dp", [(spot, spot ^ 1) for spot in range(n_dp)])
    cell_grads = spread(
        all_grad, ordered, starts, lows, by_group(rows_at), by_group(cols_at), features.shape[0]
    )
    if by_groups(n_dp):
        home, second_sum, tails, kept, far = reduce_home(
            here, swapped, later, tail, second_part, cell_grads, n_dp
        )
        first_new, first_mean_new, first_square_new, feature_grads = finish(
            home, kept, far, first_weight, first_mean, first_square, n_dp
        )
        tails = tails.reshape(n_blk, n_dp, -1, HALF)
        out_sum = tails[:, :, : -8].reshape(H, HALF)[:, :outw]
        bias_flat = tails[:, :, -8].reshape(-1)
    else:
        first_new, first_mean_new, first_square_new = adamw(
            first_weight, sum_apart(pooled, all_grad, n_blk), first_mean, first_square, rate_first
        )
        parts = lax.all_to_all(
            cell_grads.reshape(n_blk, -1, HALF), "blk", split_axis=0, concat_axis=0, tiled=True
        ).astype(jnp.float32)
        feature_grads = jnp.concatenate((parts[0] + parts[1], parts[2] + parts[3]), axis=1)
        second_sum = lax.psum_scatter(second_part, "blk", scatter_dimension=1, tiled=True)
        second_sum = second_sum.astype(jnp.float32)
        tails = lax.psum(tail, ("dp", "blk"))
        out_sum = tails[:, : H // n_blk].reshape(H, HALF)[:, :outw]
        bias_flat = tails[:, H // n_blk :].reshape(-1)
    bias_sum = bias_flat[: biases.shape[0]]
    total_loss = bias_flat[biases.shape[0]]

    second_new, second_mean_new, second_square_new = adamw(
        second_weight, second_sum, second_mean, second_square, rate_second
    )
    out_new, out_mean_new, out_square_new = adamw(
        out_weight, out_sum, out_mean, out_square, rate_out
    )
    bias_new, bias_mean_new, bias_square_new = adamw(
        biases, bias_sum, bias_mean, bias_square, rate_bias
    )
    return (
        feature_grads,
        total_loss,
        first_new,
        first_mean_new,
        first_square_new,
        second_new,
        second_mean_new,
        second_square_new,
        out_new,
        out_mean_new,
        out_square_new,
        bias_new,
        bias_mean_new,
        bias_square_new,
    )


def solution(mesh):
    in_specs = (
        P("dp", None),
        P(None, ("dp", "blk")),
        P(None, "dp"),
        P(None, ("dp", "blk")),
        P("dp", "blk"),
        P("dp", "blk"),
        P("dp", "blk"),
        P("dp", "blk"),
        P("dp", "blk"),
        P("dp", "blk"),
        P(),
        P(),
        P(),
        P(),
        P(),
        P(),
    )
    out_specs = (
        P(("dp", "blk"), None),
        P(),
        P("dp", "blk"),
        P("dp", "blk"),
        P("dp", "blk"),
        P("dp", "blk"),
        P("dp", "blk"),
        P("dp", "blk"),
        P(),
        P(),
        P(),
        P(),
        P(),
        P(),
    )
    return jax.shard_map(
        functools.partial(on_device, n_dp=mesh.shape["dp"], n_blk=mesh.shape["blk"]),
        mesh=mesh,
        in_specs=in_specs,
        out_specs=out_specs,
        check_vma=False,
    )
```

time: 3320 us -> 358 us (0.11)
  blocking collectives: 2230 us -> 0 us
  other arithmetic: 516 us -> 12.5 us
  local copies, waits for them, and re-layouts: 330 us -> 12 us
  Pallas kernels: 0 us -> 293 us
  waiting for transfers between devices: 142 us -> 16.3 us
  matrix products: 72.5 us -> 1.94 us
    unnamed x1 -> x0, blocking collectives: 2120 us -> none
    scatter-add x4 -> x0, other arithmetic: 429 us -> none  [the longest x3 323 us: on_device(): jax.ops.segment_sum(weights[corner][:, None] * grad_rows, indices[corner]...]
    pallas_call x0 -> x7, Pallas kernels: none -> 293 us  [the longest x1 78.7 us: reduce_home(): pl.pallas_call(functools.partial(reduce_kernel, n_dp), out_shape=(jax.Sha...]
    gather x4 -> x0, local copies, waits for them, and re-layouts: 140 us -> none  [the longest x3 105 us: on_device(): features[indices[corner]].astype(jnp.float32)]
    convert_element_type x10 -> x12, local copies, waits for them, and re-layouts: 112 us -> 1.48 us  [the longest x3 0.65 us: axis_points(): limit_max = (grid_side - 1).astype(jnp.float32)[:, None]]
    all_gather x3 -> x1, waiting for transfers between devices: 102 us -> 7.61 us  [gather_quarter(): gathered = lax.all_gather(ahead, 'dp', axis=0, tiled=True)]
    psum x2 -> x0, blocking collectives: 85.1 us -> none  [the longest x1 45.4 us: on_device(): lax.psum(jnp.sum(roi_table[7].astype(jnp.float32)), ('dp', 'blk'))]
    dot_general x9 -> x1, matrix products: 72.5 us -> 1.94 us  [sort_rois(): lax.dot_general(pick, rows, (((1,), (1,)), ((), ())), precision=lax.Preci...]
  transfers between devices with their start and end apart: 7 -> 5, of which waited for: 2 -> 3; matrix products, arithmetic and copies ran while one was open for 25% -> 4% of each run, Pallas kernels for 0% -> 36%
where the time goes in v1:
time: 358 us; the launch traced here: 356 us
  Pallas kernels  293 us (82%)
  waiting for transfers between devices  16.3 us (5%)
  between operations  14.6 us (4%)
  other arithmetic  12.5 us (3%)
  local copies, waits for them, and re-layouts  12 us (3%)
  starting transfers between devices  5.61 us (2%)
    pallas_call x1, Pallas kernels, reduce_home(): pl.pallas_call(functools.partial(reduce_kernel, n_dp), out_shape=(jax.Sha...  78.7 us
    pallas_call x1, Pallas kernels, middle(): pl.pallas_call(functools.partial(middle_kernel, n_dp), out_shape=(jax.Sha...  71.8 us
    pallas_call x1, Pallas kernels, spread(): pl.pallas_call(spread_kernel, out_shape=jax.ShapeDtypeStruct((cells, HALF...  61.6 us
    pallas_call x1, Pallas kernels, pool(): pl.pallas_call(pool_kernel, out_shape=jax.ShapeDtypeStruct((count, KQ), j...  51.1 us
    pallas_call x1, Pallas kernels, weight_grad(): pl.pallas_call(functools.partial(weight_grad_kernel, n_dp), grid=(SLOTS /...  15.6 us
    pallas_call x1, Pallas kernels, finish(): pl.pallas_call(finish_kernel, grid=(steps,), out_shape=(shape, shape, sha...  10.9 us
    all_to_all x1, waiting for transfers between devices, gather_quarter(): lax.all_to_all(dealt, 'blk', split_axis=0, concat_axis=0, tiled=True)  7.8 us
    all_gather x1, waiting for transfers between devices, gather_quarter(): gathered = lax.all_gather(ahead, 'dp', axis=0, tiled=True)  7.61 us
  transfers between devices with their start and end apart: 5, of which 3 were waited for; matrix products, arithmetic and copies ran while one was open for 4% of the time, Pallas kernels for 36%

profile of v1, /device:TPU:7, one launch (start us, length us, event | category | flops | bytes accessed | tf_op | source)
XLA Modules:
  0.0 355.6 jit_solution(3722317434812564815)
XLA Ops:
  10.7 2.9 deal_rows.1
  13.5 4.3 %all-to-all-start = ((bf16[4,448,256]{2,1,0:T(8,128)(2,1)}), bf16[4,448,256]{2,1,0:T(8,128)(2,1)S(1)}, u32[]{:S(2)}, u32[]{:S(2)}) async-start(bf16[4,448,256]{2,1,0:T(8,128)(2,1)} %deal_rows.1), calls=%async_computation | async-start | bytes 1835008 | tf_op jit(solution)/shard_map/all_to_all | solution.py:484
  19.9 0.8 pad.33.predict_ref
  21.2 7.8 %all-to-all-done = bf16[4,448,256]{2,1,0:T(8,128)(2,1)S(1)} async-done(((bf16[4,448,256]{2,1,0:T(8,128)(2,1)}), bf16[4,448,256]{2,1,0:T(8,128)(2,1)S(1)}, u32[]{:S(2)}, u32[]{:S(2)}) %all-to-all-start) | async-done | bytes 917536 | tf_op jit(solution)/shard_map/all_to_all | solution.py:484
  29.1 0.8 convert_reduce_fusion
  30.2 0.9 pad_maximum_fusion
  31.1 1.9 fusion.2
  35.9 0.9 maximum_minimum_fusion.1
  36.8 1.0 select_maximum_fusion.uv_ref
  37.9 51.1 %pool_bins.1.pooled_hbm.pooled_ref = bf16[1024,3328]{1,0:T(8,128)(2,1)} custom-call(s32[17]{0:T(128)} %convert_reduce_fusion.1.starts, s32[32]{0:T(128)} %reshape.375.lows, s32[3]{0:T(128)} %pad_add_fusion.meta, bf16[21760,256]{1,0:T(8,128)(2,1)} %feat_hbm.1, f32[1024,128]{1,0:T(8,128)} %select_maximum_fusion.uv_ref), custom_call_target="tpu_custom_call" | custom-call | flops 40000000000 | bytes 13000000 | tf_op jit(solution)/shard_map/pool_bins/pallas_call | solution.py:236
  92.1 0.9 concatenate.25.aux_ref
  93.6 7.6 %all-gather.2.cloned.1.call-done.ahead_hbm = bf16[3840,512]{1,0:T(8,128)(2,1)} async-done(((bf16[480,512]{1,0:T(8,128)(2,1)}), bf16[3840,512]{1,0:T(8,128)(2,1)}) %all-gather.2.cloned.1.call-update) | async-done | bytes 3932176 | tf_op jit(solution)/shard_map/all_gather | solution.py:493
  101.2 1.2 broadcast_in_dim.39.valid_ref
  102.4 71.8 %middle.1 = (bf16[1024,1024]{1,0:T(8,128)(2,1)}, bf16[1024,1024]{1,0:T(8,128)(2,1)}, f32[4,8,40,128]{3,2,1,0:T(8,128)}, bf16[3328,1024]{1,0:T(8,128)(2,1)}) custom-call(bf16[1024,3328]{1,0:T(8,128)(2,1)} %pool_bins.1.pooled_hbm.pooled_ref, bf16[3840,512]{1,0:T(8,128)(2,1)} %all-gather.2.cloned.1.call-done.ahead_hbm, bf16[416,512]{1,0:T(8,128)(2,1)} %copy-done.4, ...), custom_call_target="tpu_custom_call" | custom-call | flops 8999999488 | bytes 25000000 | tf_op jit(solution)/shard_map/middle/pallas_call | solution.py:1062
  174.2 15.6 %weight_grad.1 = (bf16[1664,1024]{1,0:T(8,128)(2,1)}, bf16[1152,1024]{1,0:T(8,128)(2,1)}, bf16[512,1024]{1,0:T(8,128)(2,1)}) custom-call(s32[3]{0:T(128)} %pad_add_fusion.meta, bf16[1024,3328]{1,0:T(8,128)(2,1)} %pool_bins.1.pooled_hbm.pooled_ref, bf16[1024,1024]{1,0:T(8,128)(2,1)} %get-tuple-element.66.grad_ref), custom_call_target="tpu_custom_call" | custom-call | flops 7000000000 | bytes 16000000 | tf_op jit(solution)/shard_map/weight_grad/pallas_call | solution.py:1173
  189.8 1.2 collective-permute-start.1
  191.0 61.6 %spread_bins.1.cells_hbm = bf16[21760,128]{1,0:T(8,128)(2,1)} custom-call(s32[17]{0:T(128)} %convert_reduce_fusion.1.starts, s32[32]{0:T(128)} %reshape.375.lows, bf16[1024,1024]{1,0:T(8,128)(2,1)} %get-tuple-element.66.grad_ref, bf16[3328,1024]{1,0:T(8,128)(2,1)} %get-tuple-element.72.weight_hbm, f32[64,512]{1,0:T(8,128)} %pad.34.row_ref, ...), custom_call_target="tpu_custom_call" | custom-call | flops 40000000000 | bytes 15000000 | tf_op jit(solution)/shard_map/spread_bins/pallas_call | solution.py:359
  252.6 0.9 collective-permute-done.1.swapped_hbm
  253.6 78.7 %reduce_home.1 = (bf16[1664,256]{1,0:T(8,128)(2,1)}, f32[128,256]{1,0:T(8,128)}, f32[1280,128]{1,0:T(8,128)}, f32[5440,128]{1,0:T(8,128)}, bf16[5440,128]{1,0:T(8,128)(2,1)}) custom-call(bf16[1664,1024]{1,0:T(8,128)(2,1)} %get-tuple-element.67.here_hbm, bf16[1152,1024]{1,0:T(8,128)(2,1)} %collective-permute-done.1.swapped_hbm, ...), custom_call_target="tpu_custom_call" | custom-call | flops 60000002048 | bytes 200000000 | tf_op jit(solution)/shard_map/reduce_home/pallas_call | solution.py:1593
  332.3 1.2 slice.203
  333.5 0.9 slice.201
  335.9 1.1 multiply_subtract_fusion
  337.0 0.8 multiply_subtract_fusion.1
  337.8 10.9 %finish.1 = (f32[1568,256]{1,0:T(8,128)}, f32[1568,256]{1,0:T(8,128)}, f32[1568,256]{1,0:T(8,128)}, f32[5440,256]{1,0:T(8,128)}) custom-call(s32[392]{0:T(512)} %constant.240.clone.table, bf16[1664,256]{1,0:T(8,128)(2,1)} %get-tuple-element.73.home_ref, f32[1568,256]{1,0:T(8,128)} %weight_ref.3, f32[1568,256]{1,0:T(8,128)} %mean_ref.1, ...), custom_call_target="tpu_custom_call" | custom-call | tf_op jit(solution)/shard_map/finish/pallas_call | solution.py:1703
  (130 shorter events, 14.2 us)
Async XLA Ops:
  7.2 10.7 %copy-start.15 = (s32[2,4]{1,0:T(2,128)S(1)}, s32[2,4]{1,0:T(2,128)}, u32[]{:S(2)}) copy-start(s32[2,4]{1,0:T(2,128)} %param.26) | copy-start | bytes 100
  7.2 10.8 %copy-start.10 = (f32[2133]{0:T(1024)S(1)}, f32[2133]{0:T(1024)}, u32[]{:S(2)}) copy-start(f32[2133]{0:T(1024)} %param.37) | copy-start | bytes 25600
  7.2 11.5 %copy-start.2 = (f32[128,256]{1,0:T(8,128)S(1)}, f32[128,256]{1,0:T(8,128)}, u32[]{:S(2)}) copy-start(f32[128,256]{1,0:T(8,128)} %param.31) | copy-start | bytes 393220
  7.2 11.6 %copy-start = (f32[1024,85]{0,1:T(8,128)S(1)}, f32[1024,85]{0,1:T(8,128)}, u32[]{:S(2)}) copy-start(f32[1024,85]{0,1:T(8,128)} %param.34) | copy-start | bytes 1044484
  13.5 15.5 %all-to-all-start = ((bf16[4,448,256]{2,1,0:T(8,128)(2,1)}), bf16[4,448,256]{2,1,0:T(8,128)(2,1)S(1)}, u32[]{:S(2)}, u32[]{:S(2)}) async-start(bf16[4,448,256]{2,1,0:T(8,128)(2,1)} %deal_rows.1), calls=%async_computation | async-start | bytes 1835008 | tf_op jit(solution)/shard_map/all_to_all | solution.py:484
  17.9 83.3 %all-gather.2.cloned.1.call-start = ((), (), s32[]{:S(2)}) async-start(), calls=%async_computation.2 | async-start | bytes 4423680 | tf_op jit(solution)/shard_map/all_gather | solution.py:493
  19.8 13.2 %copy-start.12 = (f32[8,1024]{1,0:T(8,128)}, f32[8,1024]{1,0:T(8,128)S(1)}, u32[]{:S(2)}) copy-start(f32[8,1024]{1,0:T(8,128)S(1)} %scatter.14.bias_ref) | copy-start | bytes 98308
  30.1 58.9 %copy-start.4 = (bf16[416,512]{1,0:T(8,128)(2,1)}, bf16[416,512]{1,0:T(8,128)(2,1)S(1)}, u32[]{:S(2)}) copy-start(bf16[416,512]{1,0:T(8,128)(2,1)S(1)} %get-tuple-element.129.behind_hbm) | copy-start | bytes 1277956
  31.0 222.5 %reduce-scatter.2.cloned.1.call-start = ((), (), s32[]{:S(2)}) async-start(), calls=%async_computation.3 | async-start | bytes 2359296 | tf_op jit(solution)/shard_map/reduce_scatter | solution.py:1783
  33.4 60.1 %collective-permute-start = (bf16[416,512]{1,0:T(8,128)(2,1)S(1)}, bf16[416,512]{1,0:T(8,128)(2,1)S(1)}, u32[]{:S(2)}, u32[]{:S(2)}) collective-permute-start(bf16[416,512]{1,0:T(8,128)(2,1)S(1)} %get-tuple-element.129.behind_hbm), channel_id=1, source_target_pairs={{0,4},{4,0},{8,12},{12,8},{16,20},{20,16},{24,28},{28,24},{1,5},{5... | collective-permute-start | bytes 1277960 | tf_op jit(solution)/shard_map/ppermute | solution.py:495
  93.6 8.9 %copy-start.16 = (bf16[416,512]{1,0:T(8,128)(2,1)}, bf16[416,512]{1,0:T(8,128)(2,1)S(1)}, u32[]{:S(2)}) copy-start(bf16[416,512]{1,0:T(8,128)(2,1)S(1)} %collective-permute-done.swapped_hbm) | copy-start | bytes 1277956
  189.8 63.7 %collective-permute-start.1 = (bf16[1152,1024]{1,0:T(8,128)(2,1)}, bf16[1152,1024]{1,0:T(8,128)(2,1)}, u32[]{:S(2)}, u32[]{:S(2)}) collective-permute-start(bf16[1152,1024]{1,0:T(8,128)(2,1)} %get-tuple-element.68), channel_id=1, source_target_pairs={{0,4},{4,0},{8,12},{12,8},{16,20},{20,16},{24,28},{28,24},{1,5},{5... | collective-permute-start | bytes 7077896 | tf_op jit(solution)/shard_map/ppermute | solution.py:1786
  253.5 81.7 %copy-start.11 = (f32[2133]{0:T(1024)S(1)}, f32[2133]{0:T(1024)}, u32[]{:S(2)}) copy-start(f32[2133]{0:T(1024)} %param.37) | copy-start | bytes 25600
  253.5 81.7 %copy-start.13 = (f32[2133]{0:T(1024)S(1)}, f32[2133]{0:T(1024)}, u32[]{:S(2)}) copy-start(f32[2133]{0:T(1024)} %param.38) | copy-start | bytes 25600
  253.5 81.7 %copy-start.14 = (f32[2133]{0:T(1024)S(1)}, f32[2133]{0:T(1024)}, u32[]{:S(2)}) copy-start(f32[2133]{0:T(1024)} %param.39) | copy-start | bytes 25600
  253.5 82.3 %copy-start.1 = (f32[1024,85]{0,1:T(8,128)S(1)}, f32[1024,85]{0,1:T(8,128)}, u32[]{:S(2)}) copy-start(f32[1024,85]{0,1:T(8,128)} %param.34) | copy-start | bytes 1044484
  253.5 82.3 %copy-start.5 = (f32[1024,85]{0,1:T(8,128)S(1)}, f32[1024,85]{0,1:T(8,128)}, u32[]{:S(2)}) copy-start(f32[1024,85]{0,1:T(8,128)} %param.35) | copy-start | bytes 1044484
  253.5 82.3 %copy-start.6 = (f32[1024,85]{0,1:T(8,128)S(1)}, f32[1024,85]{0,1:T(8,128)}, u32[]{:S(2)}) copy-start(f32[1024,85]{0,1:T(8,128)} %param.36) | copy-start | bytes 1044484
  332.3 4.7 %copy-start.3 = (f32[128,256]{1,0:T(8,128)S(1)}, f32[128,256]{1,0:T(8,128)}, u32[]{:S(2)}) copy-start(f32[128,256]{1,0:T(8,128)} %param.31) | copy-start | bytes 393220
  332.3 4.7 %copy-start.7 = (f32[128,256]{1,0:T(8,128)S(1)}, f32[128,256]{1,0:T(8,128)}, u32[]{:S(2)}) copy-start(f32[128,256]{1,0:T(8,128)} %param.32) | copy-start | bytes 393220
  332.3 4.7 %copy-start.8 = (f32[128,256]{1,0:T(8,128)S(1)}, f32[128,256]{1,0:T(8,128)}, u32[]{:S(2)}) copy-start(f32[128,256]{1,0:T(8,128)} %param.33) | copy-start | bytes 393220
  332.3 4.7 %copy-start.9 = (f32[128,256]{1,0:T(8,128)S(1)}, f32[128,256]{1,0:T(8,128)}, u32[]{:S(2)}) copy-start(f32[128,256]{1,0:T(8,128)} %get-tuple-element.81) | copy-start | bytes 393220
Sparse Core Ops, SparseCore 0:
  31.2 69.9 all-gather.1
  174.3 70.3 reduce-scatter.1

commit v2 on v1

--- a/solution.py
+++ b/solution.py
@@ -23,7 +23,8 @@
 KQ = SLOTS * HALF
 FAR = -1.0e6
 BATCH = 16
-LANES = 512
+MAIN = 24
+LANES = MAIN * BATCH
 SIDES = (128, 64, 32, 16)
 BASES = (0, 16384, 20480, 21504)
 WIN_ROWS = (52, 28, 16, 16)
@@ -34,7 +35,7 @@
 OWNED = 13
 SHARD = OWNED + 1
 AHEAD = H // 2
-SWAPPED = 9
+SWAPPED = 8
 LATER = OWNED - SWAPPED
 AHEAD_ROWS = (OWNED + 2) * GROUP
 MESH = pl.DeviceIdType.MESH
@@ -266,6 +267,8 @@
     weight_hbm,
     row_ref,
     col_ref,
+    last_row_ref,
+    last_col_ref,
     out_ref,
     weight_ref,
     pooled,
@@ -293,7 +296,6 @@
         return carry
 
     lax.fori_loop(0, KQ // 256, back_dot, 0)
-    right[SLOTS * BATCH :, :] = jnp.zeros((LANES - SLOTS * BATCH, HALF), jnp.bfloat16)
 
     def visit(level, begin, end, row_low, col_low):
         side, base = SIDES[level], BASES[level]
@@ -309,32 +311,56 @@
 
         lax.fori_loop(0, height, wipe, 0)
 
+        def accumulate(row_at, col_at, lanes, samples):
+            row_hat[:, :lanes] = hat(
+                row_at - lax.broadcasted_iota(jnp.int32, (56, lanes), 0).astype(jnp.float32)
+            )
+            col_hat = hat(
+                col_at - lax.broadcasted_iota(jnp.int32, (width, lanes), 0).astype(jnp.float32)
+            )
+            for row in range(0, height, chunk):
+                left = jnp.concatenate(
+                    [
+                        col_hat * row_hat[row + one : row + one + 1, :lanes]
+                        for one in range(chunk)
+                    ],
+                    axis=0,
+                ).astype(jnp.bfloat16)
+                rows = slice(row * width, (row + chunk) * width)
+                part[rows, :] += jnp.dot(left, samples, preferred_element_type=jnp.float32)
+
+        def placed(roi, row_line, col_line):
+            mine = (roi >= begin) & (roi < end)
+            return (
+                jnp.where(mine, row_line, FAR) - row_shift,
+                jnp.where(mine, col_line, FAR) - col_shift,
+            )
+
         def group(step, carry):
             first = pl.multiple_of(step * BATCH, BATCH)
-            for slot in range(SLOTS):
+            for slot in range(MAIN):
                 right[slot * BATCH : (slot + 1) * BATCH, :] = pooled[
                     pl.ds(first, BATCH), slot * HALF : (slot + 1) * HALF
                 ]
             lane = lax.broadcasted_iota(jnp.int32, (1, LANES), 1)
             roi = first + jnp.bitwise_and(lane, BATCH - 1)
-            mine = (roi >= begin) & (roi < end)
-            row_at = jnp.where(mine, row_ref[pl.ds(step, 1), :], FAR) - row_shift
-            col_at = jnp.where(mine, col_ref[pl.ds(step, 1), :], FAR) - col_shift
-            row_hat[...] = hat(
-                row_at - lax.broadcasted_iota(jnp.int32, (56, LANES), 0).astype(jnp.float32)
-            )
-            col_hat = hat(
-                col_at - lax.broadcasted_iota(jnp.int32, (width, LANES), 0).astype(jnp.float32)
-            )
-            for row in range(0, height, chunk):
-                left = jnp.concatenate(
-                    [col_hat * row_hat[row + one : row + one + 1, :] for one in range(chunk)], axis=0
-                ).astype(jnp.bfloat16)
-                rows = slice(row * width, (row + chunk) * width)
-                part[rows, :] += jnp.dot(left, right[...], preferred_element_type=jnp.float32)
+            line = pl.ds(step, 1)
+            row_at, col_at = placed(roi, row_ref[line, :], col_ref[line, :])
+            accumulate(row_at, col_at, LANES, right[...])
             return carry
 
         lax.fori_loop(begin // BATCH, (end + BATCH - 1) // BATCH, group, 0)
+
+        def last_slot(step, carry):
+            first = pl.multiple_of(step * HALF, HALF)
+            roi = first + lax.broadcasted_iota(jnp.int32, (1, HALF), 1)
+            line = pl.ds(step, 1)
+            row_at, col_at = placed(roi, last_row_ref[line, :], last_col_ref[line, :])
+            samples = pooled[pl.ds(first, HALF), MAIN * HALF : (MAIN + 1) * HALF]
+            accumulate(row_at, col_at, HALF, samples)
+            return carry
+
+        lax.fori_loop(begin // HALF, (end + HALF - 1) // HALF, last_slot, 0)
 
         def flush(row, carry):
             target = pl.ds(base + (row_low + row) * side + col_low, width)
@@ -354,7 +380,7 @@
     lax.fori_loop(0, total // 128, narrow, 0)
 
 
-def spread(first_grad, weight, starts, lows, rows_at, cols_at, cells):
+def spread(first_grad, weight, starts, lows, points, cells):
     count = first_grad.shape[0]
     return pl.pallas_call(
         spread_kernel,
@@ -364,6 +390,8 @@
             pl.BlockSpec(memory_space=pltpu.SMEM),
             pl.BlockSpec(memory_space=pltpu.VMEM),
             pl.BlockSpec(memory_space=pl.ANY),
+            pl.BlockSpec(memory_space=pltpu.VMEM),
+            pl.BlockSpec(memory_space=pltpu.VMEM),
             pl.BlockSpec(memory_space=pltpu.VMEM),
             pl.BlockSpec(memory_space=pltpu.VMEM),
         ],
@@ -382,7 +410,7 @@
             flops=40_000_000_000, bytes_accessed=15_000_000, transcendentals=0
         ),
         name="spread_bins",
-    )(starts, lows, first_grad, weight, rows_at, cols_at)
+    )(starts, lows, first_grad, weight, *points)
 
 
 def adamw(weight, gradient, moment, square, step_rate):
@@ -608,7 +636,6 @@
     predict_ref,
     bias_ref,
     aux_ref,
-    valid_ref,
     all_grad,
     second_out,
     tail_ref,
@@ -774,7 +801,7 @@
     pl.semaphore_wait(barrier, 3 + len(peers))
     counts = [
         pltpu.make_async_remote_copy(
-            src_ref=valid_ref,
+            src_ref=aux_ref.at[pl.ds(0, 8), :],
             dst_ref=valid_came.at[index],
             send_sem=valid_send.at[index],
             recv_sem=valid_recv.at[index],
@@ -945,10 +972,11 @@
     is_logit = lane < CLASSES
     is_delta = (lane >= CLASSES) & (lane < CLASSES + 4)
     label = aux_ref[:, 0:1]
-    valid_total = valid_ref[0:1, 0:1]
+    count_lane = slice(CLASSES + 4, CLASSES + 5)
+    valid_total = aux_ref[0:1, count_lane]
     for index, copy in enumerate(counts):
         copy.wait_recv()
-        valid_total = valid_total + valid_came[index, 0:1, 0:1]
+        valid_total = valid_total + valid_came[index, 0:1, count_lane]
     share = aux_ref[:, 1:2] / jnp.maximum(valid_total, 1.0)
     foreground = (label > 0.5).astype(jnp.float32)
     onehot = (lane.astype(jnp.float32) == label).astype(jnp.float32)
@@ -1053,7 +1081,7 @@
         copy.wait_send()
 
 
-def middle(pooled, ahead, behind, swapped, predict, bias, aux, valid_here, n_dp):
+def middle(pooled, ahead, behind, swapped, predict, bias, aux, n_dp):
     count = pooled.shape[0]
     rows = aux.shape[0]
     tail = (4, n_dp, 40, HALF) if by_groups(n_dp) else (4, H // 4 + 8, HALF)
@@ -1067,7 +1095,7 @@
             jax.ShapeDtypeStruct(tail, jnp.float32),
             jax.ShapeDtypeStruct((KQ, H), jnp.bfloat16),
         ),
-        in_specs=[any_spec] * 4 + [vmem_spec] * 4,
+        in_specs=[any_spec] * 4 + [vmem_spec] * 3,
         out_specs=(any_spec, vmem_spec, vmem_spec, any_spec),
         scratch_shapes=[
             pltpu.VMEM((count, KQ), jnp.bfloat16),
@@ -1107,7 +1135,7 @@
             flops=9_000_000_000, bytes_accessed=25_000_000, transcendentals=1_500_000
         ),
         name="middle",
-    )(pooled, ahead, behind, swapped, predict, bias, aux, valid_here)
+    )(pooled, ahead, behind, swapped, predict, bias, aux)
 
 
 def weight_grad_kernel(n_dp, meta, pooled_ref, grad_ref, here_hbm, there_hbm, later_hbm, stage, sems):
@@ -1746,7 +1774,7 @@
     outw = out_weight.shape[1]
     rois = jnp.concatenate((roi_table.astype(jnp.float32), box_targets), axis=0)
     weight, all_rois = gather_quarter(first_weight, second_weight, rois, n_dp)
-    valid_here = jnp.broadcast_to(jnp.sum(all_rois[7]), (8, HALF))
+    valid_here = jnp.sum(all_rois[7])
     if not by_groups(n_dp):
         valid_here = lax.psum(valid_here, "dp")
     predict = jnp.pad(out_weight.astype(jnp.bfloat16), ((0, 0), (0, HALF - outw)))
@@ -1760,8 +1788,7 @@
     points = jnp.concatenate((jnp.pad(row_sevens, apart), jnp.pad(col_sevens, apart)), axis=1)
 
     def by_group(values):
-        grouped = values.reshape(-1, BATCH, SLOTS).transpose(0, 2, 1).reshape(-1, SLOTS * BATCH)
-        return jnp.pad(grouped, ((0, 0), (0, LANES - SLOTS * BATCH)), constant_values=FAR)
+        return values[:, :MAIN].reshape(-1, BATCH, MAIN).transpose(0, 2, 1).reshape(-1, LANES)
 
     my_table = lax.dynamic_slice_in_dim(table, place * roi_count, roi_count, axis=1)
     my_targets = lax.dynamic_slice_in_dim(targets, place * roi_count, roi_count, axis=0)
@@ -1771,21 +1798,32 @@
             my_table[7].astype(jnp.float32)[:, None],
             jnp.zeros((roi_count, CLASSES - 2), jnp.float32),
             my_targets,
-            jnp.zeros((roi_count, HALF - CLASSES - 4), jnp.float32),
+            jnp.broadcast_to(valid_here, (roi_count, 1)),
+            jnp.zeros((roi_count, HALF - CLASSES - 5), jnp.float32),
         ),
         axis=1,
     )
     meta = jnp.stack((half, parity, lax.axis_index("dp") % 2))
     pooled = pool(features, meta, starts, lows, points)
     all_grad, second_wgrad, tail, ordered = middle(
-        pooled, *weight, predict, bias, aux, valid_here, n_dp
+        pooled, *weight, predict, bias, aux, n_dp
     )
     second_part = lax.psum_scatter(second_wgrad, "dp", scatter_dimension=0, tiled=True)
     if by_groups(n_dp):
         here, there, later = weight_grad(pooled, all_grad, meta, n_dp)
         swapped = lax.ppermute(there, "dp", [(spot, spot ^ 1) for spot in range(n_dp)])
     cell_grads = spread(
-        all_grad, ordered, starts, lows, by_group(rows_at), by_group(cols_at), features.shape[0]
+        all_grad,
+        ordered,
+        starts,
+        lows,
+        (
+            by_group(rows_at),
+            by_group(cols_at),
+            rows_at[:, MAIN].reshape(-1, HALF),
+            cols_at[:, MAIN].reshape(-1, HALF),
+        ),
+        features.shape[0],
     )
     if by_groups(n_dp):
         home, second_sum, tails, kept, far = reduce_home(

time: 358 us -> 361 us (level)
    pallas_call x1, Pallas kernels: 61.6 us -> 65.3 us  [spread(): pl.pallas_call(spread_kernel, out_shape=jax.ShapeDtypeStruct((cells, HALF...]
  transfers between devices with their start and end apart: 5 -> 5, of which waited for: 3 -> 2; matrix products, arithmetic and copies ran while one was open for 4% -> 4% of each run, Pallas kernels for 36% -> 37%
where the time goes in v2:
time: 361 us; the launch traced here: 356 us
  Pallas kernels  294 us (81%)
  waiting for transfers between devices  16.6 us (5%)
  between operations  14.6 us (4%)
  other arithmetic  11.9 us (3%)
  local copies, waits for them, and re-layouts  11 us (3%)
  starting transfers between devices  5.55 us (2%)
    pallas_call x1, Pallas kernels, reduce_home(): pl.pallas_call(functools.partial(reduce_kernel, n_dp), out_shape=(jax.Sha...  76.6 us
    pallas_call x1, Pallas kernels, middle(): pl.pallas_call(functools.partial(middle_kernel, n_dp), out_shape=(jax.Sha...  71.7 us
    pallas_call x1, Pallas kernels, spread(): pl.pallas_call(spread_kernel, out_shape=jax.ShapeDtypeStruct((cells, HALF...  65.3 us
    pallas_call x1, Pallas kernels, pool(): pl.pallas_call(pool_kernel, out_shape=jax.ShapeDtypeStruct((count, KQ), j...  51.3 us
    pallas_call x1, Pallas kernels, weight_grad(): pl.pallas_call(functools.partial(weight_grad_kernel, n_dp), grid=(SLOTS /...  15.6 us
    pallas_call x1, Pallas kernels, finish(): pl.pallas_call(finish_kernel, grid=(steps,), out_shape=(shape, shape, sha...  10.9 us
    all_gather x1, waiting for transfers between devices, gather_quarter(): gathered = lax.all_gather(ahead, 'dp', axis=0, tiled=True)  8.34 us
    all_to_all x1, waiting for transfers between devices, gather_quarter(): lax.all_to_all(dealt, 'blk', split_axis=0, concat_axis=0, tiled=True)  8.22 us
  transfers between devices with their start and end apart: 5, of which 2 were waited for; matrix products, arithmetic and copies ran while one was open for 4% of the time, Pallas kernels for 37%

profile of v2, /device:TPU:7, one launch (start us, length us, event | category | flops | bytes accessed | tf_op | source)
XLA Modules:
  0.0 355.9 jit_solution(7387849370527385613)
XLA Ops:
  10.7 2.9 deal_rows.1
  13.5 4.3 %all-to-all-start = ((bf16[4,448,256]{2,1,0:T(8,128)(2,1)}), bf16[4,448,256]{2,1,0:T(8,128)(2,1)S(1)}, u32[]{:S(2)}, u32[]{:S(2)}) async-start(bf16[4,448,256]{2,1,0:T(8,128)(2,1)} %deal_rows.1), calls=%async_computation | async-start | bytes 1835008 | tf_op jit(solution)/shard_map/all_to_all | solution.py:512
  19.4 0.8 pad.26.predict_ref
  20.8 8.2 %all-to-all-done = bf16[4,448,256]{2,1,0:T(8,128)(2,1)S(1)} async-done(((bf16[4,448,256]{2,1,0:T(8,128)(2,1)}), bf16[4,448,256]{2,1,0:T(8,128)(2,1)S(1)}, u32[]{:S(2)}, u32[]{:S(2)}) %all-to-all-start) | async-done | bytes 917536 | tf_op jit(solution)/shard_map/all_to_all | solution.py:512
  29.3 0.9 pad_maximum_fusion
  30.3 0.8 convert_reduce_fusion
  31.1 1.9 fusion.2
  35.3 0.9 maximum_minimum_fusion.1
  36.1 1.0 select_maximum_fusion.uv_ref
  37.1 51.3 %pool_bins.1.pooled_hbm.pooled_ref = bf16[1024,3328]{1,0:T(8,128)(2,1)} custom-call(s32[17]{0:T(128)} %convert_reduce_fusion.1.starts, s32[32]{0:T(128)} %reshape.291.lows, s32[3]{0:T(128)} %pad_add_fusion.meta, bf16[21760,256]{1,0:T(8,128)(2,1)} %feat_hbm.1, f32[1024,128]{1,0:T(8,128)} %select_maximum_fusion.uv_ref), custom_call_target="tpu_custom_call" | custom-call | flops 40000000000 | bytes 13000000 | tf_op jit(solution)/shard_map/pool_bins/pallas_call | solution.py:237
  89.4 0.8 copy.87.row_ref
  90.7 0.8 copy.88.col_ref
  92.8 0.9 concatenate.25.aux_ref
  93.7 8.3 %all-gather.2.cloned.1.call-done.ahead_hbm = bf16[3840,512]{1,0:T(8,128)(2,1)} async-done(((bf16[480,512]{1,0:T(8,128)(2,1)}), bf16[3840,512]{1,0:T(8,128)(2,1)}) %all-gather.2.cloned.1.call-update) | async-done | bytes 3932176 | tf_op jit(solution)/shard_map/all_gather | solution.py:521
  102.0 71.7 %middle.1 = (bf16[1024,1024]{1,0:T(8,128)(2,1)}, bf16[1024,1024]{1,0:T(8,128)(2,1)}, f32[4,8,40,128]{3,2,1,0:T(8,128)}, bf16[3328,1024]{1,0:T(8,128)(2,1)}) custom-call(bf16[1024,3328]{1,0:T(8,128)(2,1)} %pool_bins.1.pooled_hbm.pooled_ref, bf16[3840,512]{1,0:T(8,128)(2,1)} %all-gather.2.cloned.1.call-done.ahead_hbm, bf16[416,512]{1,0:T(8,128)(2,1)} %copy-done.4, ...), custom_call_target="tpu_custom_call" | custom-call | flops 8999999488 | bytes 25000000 | tf_op jit(solution)/shard_map/middle/pallas_call | solution.py:1090
  173.8 15.6 %weight_grad.1 = (bf16[1664,1024]{1,0:T(8,128)(2,1)}, bf16[1024,1024]{1,0:T(8,128)(2,1)}, bf16[640,1024]{1,0:T(8,128)(2,1)}) custom-call(s32[3]{0:T(128)} %pad_add_fusion.meta, bf16[1024,3328]{1,0:T(8,128)(2,1)} %pool_bins.1.pooled_hbm.pooled_ref, bf16[1024,1024]{1,0:T(8,128)(2,1)} %get-tuple-element.66.grad_ref), custom_call_target="tpu_custom_call" | custom-call | flops 7000000000 | bytes 16000000 | tf_op jit(solution)/shard_map/weight_grad/pallas_call | solution.py:1201
  189.4 1.2 collective-permute-start.1
  190.6 65.3 %spread_bins.1.cells_hbm = bf16[21760,128]{1,0:T(8,128)(2,1)} custom-call(s32[17]{0:T(128)} %convert_reduce_fusion.1.starts, s32[32]{0:T(128)} %reshape.291.lows, bf16[1024,1024]{1,0:T(8,128)(2,1)} %get-tuple-element.66.grad_ref, bf16[3328,1024]{1,0:T(8,128)(2,1)} %get-tuple-element.72.weight_hbm, f32[64,384]{1,0:T(8,128)} %copy.87.row_ref, ...), custom_call_target="tpu_custom_call" | custom-call | flops 40000000000 | bytes 15000000 | tf_op jit(solution)/shard_map/spread_bins/pallas_call | solution.py:385
  256.0 76.6 %reduce_home.1 = (bf16[1664,256]{1,0:T(8,128)(2,1)}, f32[128,256]{1,0:T(8,128)}, f32[1280,128]{1,0:T(8,128)}, f32[5440,128]{1,0:T(8,128)}, bf16[5440,128]{1,0:T(8,128)(2,1)}) custom-call(bf16[1664,1024]{1,0:T(8,128)(2,1)} %get-tuple-element.67.here_hbm, bf16[1024,1024]{1,0:T(8,128)(2,1)} %collective-permute-done.1.swapped_hbm, ...), custom_call_target="tpu_custom_call" | custom-call | flops 60000002048 | bytes 200000000 | tf_op jit(solution)/shard_map/reduce_home/pallas_call | solution.py:1621
  332.7 1.2 slice.223
  333.8 0.9 slice.221
  336.2 1.1 multiply_subtract_fusion
  337.4 0.8 multiply_subtract_fusion.1
  338.2 10.9 %finish.1 = (f32[1568,256]{1,0:T(8,128)}, f32[1568,256]{1,0:T(8,128)}, f32[1568,256]{1,0:T(8,128)}, f32[5440,256]{1,0:T(8,128)}) custom-call(s32[392]{0:T(512)} %constant.240.clone.table, bf16[1664,256]{1,0:T(8,128)(2,1)} %get-tuple-element.73.home_ref, f32[1568,256]{1,0:T(8,128)} %weight_ref.3, f32[1568,256]{1,0:T(8,128)} %mean_ref.1, ...), custom_call_target="tpu_custom_call" | custom-call | tf_op jit(solution)/shard_map/finish/pallas_call | solution.py:1731
  (102 shorter events, 12.3 us)
Async XLA Ops:
  7.2 10.7 %copy-start.10 = (f32[2133]{0:T(1024)S(1)}, f32[2133]{0:T(1024)}, u32[]{:S(2)}) copy-start(f32[2133]{0:T(1024)} %param.37) | copy-start | bytes 25600
  7.2 10.7 %copy-start.15 = (s32[2,4]{1,0:T(2,128)S(1)}, s32[2,4]{1,0:T(2,128)}, u32[]{:S(2)}) copy-start(s32[2,4]{1,0:T(2,128)} %param.26) | copy-start | bytes 100
  7.2 11.5 %copy-start.2 = (f32[128,256]{1,0:T(8,128)S(1)}, f32[128,256]{1,0:T(8,128)}, u32[]{:S(2)}) copy-start(f32[128,256]{1,0:T(8,128)} %param.31) | copy-start | bytes 393220
  7.2 11.6 %copy-start = (f32[1024,85]{0,1:T(8,128)S(1)}, f32[1024,85]{0,1:T(8,128)}, u32[]{:S(2)}) copy-start(f32[1024,85]{0,1:T(8,128)} %param.34) | copy-start | bytes 1044484
  13.5 15.5 %all-to-all-start = ((bf16[4,448,256]{2,1,0:T(8,128)(2,1)}), bf16[4,448,256]{2,1,0:T(8,128)(2,1)S(1)}, u32[]{:S(2)}, u32[]{:S(2)}) async-start(bf16[4,448,256]{2,1,0:T(8,128)(2,1)} %deal_rows.1), calls=%async_computation | async-start | bytes 1835008 | tf_op jit(solution)/shard_map/all_to_all | solution.py:512
  17.9 84.2 %all-gather.2.cloned.1.call-start = ((), (), s32[]{:S(2)}) async-start(), calls=%async_computation.2 | async-start | bytes 4423680 | tf_op jit(solution)/shard_map/all_gather | solution.py:521
  19.4 10.8 %copy-start.12 = (f32[8,1024]{1,0:T(8,128)}, f32[8,1024]{1,0:T(8,128)S(1)}, u32[]{:S(2)}) copy-start(f32[8,1024]{1,0:T(8,128)S(1)} %scatter.14.bias_ref) | copy-start | bytes 98308
  29.2 59.2 %copy-start.4 = (bf16[416,512]{1,0:T(8,128)(2,1)}, bf16[416,512]{1,0:T(8,128)(2,1)S(1)}, u32[]{:S(2)}) copy-start(bf16[416,512]{1,0:T(8,128)(2,1)S(1)} %get-tuple-element.121.behind_hbm) | copy-start | bytes 1277956
  30.2 225.8 %reduce-scatter.2.cloned.1.call-start = ((), (), s32[]{:S(2)}) async-start(), calls=%async_computation.3 | async-start | bytes 2359296 | tf_op jit(solution)/shard_map/reduce_scatter | solution.py:1811
  34.6 59.1 %collective-permute-start = (bf16[416,512]{1,0:T(8,128)(2,1)S(1)}, bf16[416,512]{1,0:T(8,128)(2,1)S(1)}, u32[]{:S(2)}, u32[]{:S(2)}) collective-permute-start(bf16[416,512]{1,0:T(8,128)(2,1)S(1)} %get-tuple-element.121.behind_hbm), channel_id=1, source_target_pairs={{0,4},{4,0},{8,12},{12,8},{16,20},{20,16},{24,28},{28,24},{1,5},{5... | collective-permute-start | bytes 1277960 | tf_op jit(solution)/shard_map/ppermute | solution.py:523
  93.7 8.3 %copy-start.16 = (bf16[416,512]{1,0:T(8,128)(2,1)}, bf16[416,512]{1,0:T(8,128)(2,1)S(1)}, u32[]{:S(2)}) copy-start(bf16[416,512]{1,0:T(8,128)(2,1)S(1)} %collective-permute-done.swapped_hbm) | copy-start | bytes 1277956
  189.4 66.5 %collective-permute-start.1 = (bf16[1024,1024]{1,0:T(8,128)(2,1)}, bf16[1024,1024]{1,0:T(8,128)(2,1)}, u32[]{:S(2)}, u32[]{:S(2)}) collective-permute-start(bf16[1024,1024]{1,0:T(8,128)(2,1)} %get-tuple-element.68), channel_id=1, source_target_pairs={{0,4},{4,0},{8,12},{12,8},{16,20},{20,16},{24,28},{28,24},{1,5},{5... | collective-permute-start | bytes 6291464 | tf_op jit(solution)/shard_map/ppermute | solution.py:1814
  255.9 79.6 %copy-start.11 = (f32[2133]{0:T(1024)S(1)}, f32[2133]{0:T(1024)}, u32[]{:S(2)}) copy-start(f32[2133]{0:T(1024)} %param.37) | copy-start | bytes 25600
  255.9 79.6 %copy-start.13 = (f32[2133]{0:T(1024)S(1)}, f32[2133]{0:T(1024)}, u32[]{:S(2)}) copy-start(f32[2133]{0:T(1024)} %param.38) | copy-start | bytes 25600
  256.0 79.6 %copy-start.14 = (f32[2133]{0:T(1024)S(1)}, f32[2133]{0:T(1024)}, u32[]{:S(2)}) copy-start(f32[2133]{0:T(1024)} %param.39) | copy-start | bytes 25600
  256.0 80.2 %copy-start.1 = (f32[1024,85]{0,1:T(8,128)S(1)}, f32[1024,85]{0,1:T(8,128)}, u32[]{:S(2)}) copy-start(f32[1024,85]{0,1:T(8,128)} %param.34) | copy-start | bytes 1044484
  256.0 80.2 %copy-start.5 = (f32[1024,85]{0,1:T(8,128)S(1)}, f32[1024,85]{0,1:T(8,128)}, u32[]{:S(2)}) copy-start(f32[1024,85]{0,1:T(8,128)} %param.35) | copy-start | bytes 1044484
  256.0 80.2 %copy-start.6 = (f32[1024,85]{0,1:T(8,128)S(1)}, f32[1024,85]{0,1:T(8,128)}, u32[]{:S(2)}) copy-start(f32[1024,85]{0,1:T(8,128)} %param.36) | copy-start | bytes 1044484
  332.6 4.7 %copy-start.3 = (f32[128,256]{1,0:T(8,128)S(1)}, f32[128,256]{1,0:T(8,128)}, u32[]{:S(2)}) copy-start(f32[128,256]{1,0:T(8,128)} %param.31) | copy-start | bytes 393220
  332.7 4.7 %copy-start.7 = (f32[128,256]{1,0:T(8,128)S(1)}, f32[128,256]{1,0:T(8,128)}, u32[]{:S(2)}) copy-start(f32[128,256]{1,0:T(8,128)} %param.32) | copy-start | bytes 393220
  332.7 4.7 %copy-start.8 = (f32[128,256]{1,0:T(8,128)S(1)}, f32[128,256]{1,0:T(8,128)}, u32[]{:S(2)}) copy-start(f32[128,256]{1,0:T(8,128)} %param.33) | copy-start | bytes 393220
  332.7 4.7 %copy-start.9 = (f32[128,256]{1,0:T(8,128)S(1)}, f32[128,256]{1,0:T(8,128)}, u32[]{:S(2)}) copy-start(f32[128,256]{1,0:T(8,128)} %get-tuple-element.81) | copy-start | bytes 393220
Sparse Core Ops, SparseCore 0:
  30.3 71.7 all-gather.1
  173.9 70.1 reduce-scatter.1

commit v3 on v1

--- a/solution.py
+++ b/solution.py
@@ -608,7 +608,6 @@
     predict_ref,
     bias_ref,
     aux_ref,
-    valid_ref,
     all_grad,
     second_out,
     tail_ref,
@@ -774,7 +773,7 @@
     pl.semaphore_wait(barrier, 3 + len(peers))
     counts = [
         pltpu.make_async_remote_copy(
-            src_ref=valid_ref,
+            src_ref=aux_ref.at[pl.ds(0, 8), :],
             dst_ref=valid_came.at[index],
             send_sem=valid_send.at[index],
             recv_sem=valid_recv.at[index],
@@ -945,10 +944,11 @@
     is_logit = lane < CLASSES
     is_delta = (lane >= CLASSES) & (lane < CLASSES + 4)
     label = aux_ref[:, 0:1]
-    valid_total = valid_ref[0:1, 0:1]
+    count_lane = slice(CLASSES + 4, CLASSES + 5)
+    valid_total = aux_ref[0:1, count_lane]
     for index, copy in enumerate(counts):
         copy.wait_recv()
-        valid_total = valid_total + valid_came[index, 0:1, 0:1]
+        valid_total = valid_total + valid_came[index, 0:1, count_lane]
     share = aux_ref[:, 1:2] / jnp.maximum(valid_total, 1.0)
     foreground = (label > 0.5).astype(jnp.float32)
     onehot = (lane.astype(jnp.float32) == label).astype(jnp.float32)
@@ -1053,7 +1053,7 @@
         copy.wait_send()
 
 
-def middle(pooled, ahead, behind, swapped, predict, bias, aux, valid_here, n_dp):
+def middle(pooled, ahead, behind, swapped, predict, bias, aux, n_dp):
     count = pooled.shape[0]
     rows = aux.shape[0]
     tail = (4, n_dp, 40, HALF) if by_groups(n_dp) else (4, H // 4 + 8, HALF)
@@ -1067,7 +1067,7 @@
             jax.ShapeDtypeStruct(tail, jnp.float32),
             jax.ShapeDtypeStruct((KQ, H), jnp.bfloat16),
         ),
-        in_specs=[any_spec] * 4 + [vmem_spec] * 4,
+        in_specs=[any_spec] * 4 + [vmem_spec] * 3,
         out_specs=(any_spec, vmem_spec, vmem_spec, any_spec),
         scratch_shapes=[
             pltpu.VMEM((count, KQ), jnp.bfloat16),
@@ -1107,7 +1107,7 @@
             flops=9_000_000_000, bytes_accessed=25_000_000, transcendentals=1_500_000
         ),
         name="middle",
-    )(pooled, ahead, behind, swapped, predict, bias, aux, valid_here)
+    )(pooled, ahead, behind, swapped, predict, bias, aux)
 
 
 def weight_grad_kernel(n_dp, meta, pooled_ref, grad_ref, here_hbm, there_hbm, later_hbm, stage, sems):
@@ -1661,11 +1661,51 @@
     square_ref,
     kept_ref,
     far_ref,
+    tails_ref,
+    second_grad_ref,
+    second_refs_0,
+    second_refs_1,
+    second_refs_2,
+    out_refs_0,
+    out_refs_1,
+    out_refs_2,
     new_ref,
     new_mean_ref,
     new_square_ref,
     features_ref,
+    second_new_0,
+    second_new_1,
+    second_new_2,
+    out_new_0,
+    out_new_1,
+    out_new_2,
 ):
+    @pl.when(pl.program_id(0) == 0)
+    def _():
+        seconds = adamw(
+            second_refs_0[...],
+            second_grad_ref[...],
+            second_refs_1[...],
+            second_refs_2[...],
+            rate_second,
+        )
+        second_new_0[...], second_new_1[...], second_new_2[...] = seconds
+
+        def owner_step(owner, carry):
+            source = pl.ds(pl.multiple_of(owner * 40, 8), 32)
+            rows = pl.ds(pl.multiple_of(owner * 32, 32), 32)
+            outs = adamw(
+                out_refs_0[rows, :],
+                tails_ref[source, :][:, : CLASSES + 4],
+                out_refs_1[rows, :],
+                out_refs_2[rows, :],
+                rate_out,
+            )
+            out_new_0[rows, :], out_new_1[rows, :], out_new_2[rows, :] = outs
+            return carry
+
+        lax.fori_loop(0, H // 32, owner_step, 0)
+
     groups = weight_ref.shape[0] // GROUP
     span = K1 // GROUP // lax.axis_size("dp")
     base = lax.axis_index("dp") * span + pl.program_id(0) * groups
@@ -1691,7 +1731,8 @@
             )
 
 
-def finish(home, kept, far, first_weight, first_mean, first_square, n_dp):
+def finish(home, kept, far, tails, second_sum, firsts, seconds, outs, n_dp):
+    first_weight, first_mean, first_square = firsts
     cols = first_weight.shape[1]
     steps = 7
     table = jnp.asarray(group_sources(n_dp).reshape(-1))
@@ -1700,10 +1741,18 @@
     cells = kept.shape[0]
     some = -(-cells // steps // 16) * 16
     part = pl.BlockSpec((some, HALF), lambda i: (i, 0))
+
+    def whole(values):
+        return pl.BlockSpec(values.shape, lambda i: (0, 0))
+
+    others = (tails, second_sum, *seconds, *outs)
     return pl.pallas_call(
         finish_kernel,
         grid=(steps,),
-        out_shape=(shape, shape, shape, jax.ShapeDtypeStruct((cells, C), jnp.float32)),
+        out_shape=(
+            (shape, shape, shape, jax.ShapeDtypeStruct((cells, C), jnp.float32))
+            + tuple(jax.ShapeDtypeStruct(one.shape, jnp.float32) for one in (*seconds, *outs))
+        ),
         in_specs=[
             pl.BlockSpec(memory_space=pltpu.SMEM),
             pl.BlockSpec(memory_space=pltpu.VMEM),
@@ -1712,11 +1761,15 @@
             block,
             part,
             part,
+            *(whole(one) for one in others),
         ],
-        out_specs=(block, block, block, pl.BlockSpec((some, C), lambda i: (i, 0))),
+        out_specs=(
+            (block, block, block, pl.BlockSpec((some, C), lambda i: (i, 0)))
+            + tuple(whole(one) for one in (*seconds, *outs))
+        ),
         compiler_params=pltpu.CompilerParams(vmem_limit_bytes=VMEM_LIMIT),
         name="finish",
-    )(table, home, first_weight, first_mean, first_square, kept, far)
+    )(table, home, first_weight, first_mean, first_square, kept, far, *others)
 
 
 def on_device(
@@ -1746,7 +1799,7 @@
     outw = out_weight.shape[1]
     rois = jnp.concatenate((roi_table.astype(jnp.float32), box_targets), axis=0)
     weight, all_rois = gather_quarter(first_weight, second_weight, rois, n_dp)
-    valid_here = jnp.broadcast_to(jnp.sum(all_rois[7]), (8, HALF))
+    valid_here = jnp.sum(all_rois[7])
     if not by_groups(n_dp):
         valid_here = lax.psum(valid_here, "dp")
     predict = jnp.pad(out_weight.astype(jnp.bfloat16), ((0, 0), (0, HALF - outw)))
@@ -1771,14 +1824,15 @@
             my_table[7].astype(jnp.float32)[:, None],
             jnp.zeros((roi_count, CLASSES - 2), jnp.float32),
             my_targets,
-            jnp.zeros((roi_count, HALF - CLASSES - 4), jnp.float32),
+            jnp.broadcast_to(valid_here, (roi_count, 1)),
+            jnp.zeros((roi_count, HALF - CLASSES - 5), jnp.float32),
         ),
         axis=1,
     )
     meta = jnp.stack((half, parity, lax.axis_index("dp") % 2))
     pooled = pool(features, meta, starts, lows, points)
     all_grad, second_wgrad, tail, ordered = middle(
-        pooled, *weight, predict, bias, aux, valid_here, n_dp
+        pooled, *weight, predict, bias, aux, n_dp
     )
     second_part = lax.psum_scatter(second_wgrad, "dp", scatter_dimension=0, tiled=True)
     if by_groups(n_dp):
@@ -1791,11 +1845,20 @@
         home, second_sum, tails, kept, far = reduce_home(
             here, swapped, later, tail, second_part, cell_grads, n_dp
         )
-        first_new, first_mean_new, first_square_new, feature_grads = finish(
-            home, kept, far, first_weight, first_mean, first_square, n_dp
-        )
+        first_new, first_mean_new, first_square_new, feature_grads, *rest = finish(
+            home,
+            kept,
+            far,
+            tails,
+            second_sum,
+            (first_weight, first_mean, first_square),
+            (second_weight, second_mean, second_square),
+            (out_weight, out_mean, out_square),
+            n_dp,
+        )
+        second_new, second_mean_new, second_square_new = rest[:3]
+        out_new, out_mean_new, out_square_new = rest[3:]
         tails = tails.reshape(n_blk, n_dp, -1, HALF)
-        out_sum = tails[:, :, : -8].reshape(H, HALF)[:, :outw]
         bias_flat = tails[:, :, -8].reshape(-1)
     else:
         first_new, first_mean_new, first_square_new = adamw(
@@ -1810,15 +1873,15 @@
         tails = lax.psum(tail, ("dp", "blk"))
         out_sum = tails[:, : H // n_blk].reshape(H, HALF)[:, :outw]
         bias_flat = tails[:, H // n_blk :].reshape(-1)
+        second_new, second_mean_new, second_square_new = adamw(
+            second_weight, second_sum, second_mean, second_square, rate_second
+        )
+        out_new, out_mean_new, out_square_new = adamw(
+            out_weight, out_sum, out_mean, out_square, rate_out
+        )
     bias_sum = bias_flat[: biases.shape[0]]
     total_loss = bias_flat[biases.shape[0]]
 
-    second_new, second_mean_new, second_square_new = adamw(
-        second_weight, second_sum, second_mean, second_square, rate_second
-    )
-    out_new, out_mean_new, out_square_new = adamw(
-        out_weight, out_sum, out_mean, out_square, rate_out
-    )
     bias_new, bias_mean_new, bias_square_new = adamw(
         biases, bias_sum, bias_mean, bias_square, rate_bias
     )

time: 358 us -> 362 us (1.011)
  local copies, waits for them, and re-layouts: 12 us -> 20.5 us
    unnamed x38 -> x35, local copies, waits for them, and re-layouts: 0.51 us -> 10.8 us
  transfers between devices with their start and end apart: 5 -> 5, of which waited for: 3 -> 3; matrix products, arithmetic and copies ran while one was open for 4% -> 5% of each run, Pallas kernels for 36% -> 35%
where the time goes in v3:
time: 362 us; the launch traced here: 361 us
  Pallas kernels  293 us (81%)
  local copies, waits for them, and re-layouts  20.5 us (6%)
  between operations  14.6 us (4%)
  waiting for transfers between devices  14 us (4%)
  other arithmetic  10.6 us (3%)
  starting transfers between devices  5.61 us (2%)
    pallas_call x1, Pallas kernels, reduce_home(): pl.pallas_call(functools.partial(reduce_kernel, n_dp), out_shape=(jax.Sha...  78.3 us
    pallas_call x1, Pallas kernels, middle(): pl.pallas_call(functools.partial(middle_kernel, n_dp), out_shape=(jax.Sha...  71.8 us
    pallas_call x1, Pallas kernels, spread(): pl.pallas_call(spread_kernel, out_shape=jax.ShapeDtypeStruct((cells, HALF...  61 us
    pallas_call x1, Pallas kernels, pool(): pl.pallas_call(pool_kernel, out_shape=jax.ShapeDtypeStruct((count, KQ), j...  50.2 us
    pallas_call x1, Pallas kernels, weight_grad(): pl.pallas_call(functools.partial(weight_grad_kernel, n_dp), grid=(SLOTS /...  15.6 us
    pallas_call x1, Pallas kernels, finish(): pl.pallas_call(finish_kernel, grid=(steps,), out_shape=(shape, shape, sha...  13.5 us
    unnamed x35, local copies, waits for them, and re-layouts  10.8 us
    all_gather x1, waiting for transfers between devices, gather_quarter(): gathered = lax.all_gather(ahead, 'dp', axis=0, tiled=True)  7.82 us
  transfers between devices with their start and end apart: 5, of which 3 were waited for; matrix products, arithmetic and copies ran while one was open for 5% of the time, Pallas kernels for 35%

profile of v3, /device:TPU:7, one launch (start us, length us, event | category | flops | bytes accessed | tf_op | source)
XLA Modules:
  0.0 360.5 jit_solution(13953454440695098874)
XLA Ops:
  10.7 2.9 deal_rows.1
  13.6 4.3 %all-to-all-start = ((bf16[4,448,256]{2,1,0:T(8,128)(2,1)}), bf16[4,448,256]{2,1,0:T(8,128)(2,1)S(1)}, u32[]{:S(2)}, u32[]{:S(2)}) async-start(bf16[4,448,256]{2,1,0:T(8,128)(2,1)} %deal_rows.1), calls=%async_computation | async-start | bytes 1835008 | tf_op jit(solution)/shard_map/all_to_all | solution.py:484
  18.1 1.0 copy.120.out_refs_0
  20.5 1.1 copy.121.out_refs_1
  21.6 1.0 copy.122.out_refs_2
  24.4 4.7 %all-to-all-done = bf16[4,448,256]{2,1,0:T(8,128)(2,1)S(1)} async-done(((bf16[4,448,256]{2,1,0:T(8,128)(2,1)}), bf16[4,448,256]{2,1,0:T(8,128)(2,1)S(1)}, u32[]{:S(2)}, u32[]{:S(2)}) %all-to-all-start) | async-done | bytes 917536 | tf_op jit(solution)/shard_map/all_to_all | solution.py:484
  31.2 1.9 fusion.2
  36.0 0.9 maximum_minimum_fusion.1
  36.9 1.0 select_maximum_fusion.uv_ref
  37.9 50.2 %pool_bins.1.pooled_hbm.pooled_ref = bf16[1024,3328]{1,0:T(8,128)(2,1)} custom-call(s32[17]{0:T(128)} %convert_reduce_fusion.1.starts, s32[32]{0:T(128)} %reshape.372.lows, s32[3]{0:T(128)} %pad_add_fusion.meta, bf16[21760,256]{1,0:T(8,128)(2,1)} %feat_hbm.1, f32[1024,128]{1,0:T(8,128)} %select_maximum_fusion.uv_ref), custom_call_target="tpu_custom_call" | custom-call | flops 40000000000 | bytes 13000000 | tf_op jit(solution)/shard_map/pool_bins/pallas_call | solution.py:236
  92.5 0.9 concatenate.25.aux_ref
  93.4 7.8 %all-gather.2.cloned.1.call-done.ahead_hbm = bf16[3840,512]{1,0:T(8,128)(2,1)} async-done(((bf16[480,512]{1,0:T(8,128)(2,1)}), bf16[3840,512]{1,0:T(8,128)(2,1)}) %all-gather.2.cloned.1.call-update) | async-done | bytes 3932176 | tf_op jit(solution)/shard_map/all_gather | solution.py:493
  101.2 71.8 %middle.1 = (bf16[1024,1024]{1,0:T(8,128)(2,1)}, bf16[1024,1024]{1,0:T(8,128)(2,1)}, f32[4,8,40,128]{3,2,1,0:T(8,128)}, bf16[3328,1024]{1,0:T(8,128)(2,1)}) custom-call(bf16[1024,3328]{1,0:T(8,128)(2,1)} %pool_bins.1.pooled_hbm.pooled_ref, bf16[3840,512]{1,0:T(8,128)(2,1)} %all-gather.2.cloned.1.call-done.ahead_hbm, bf16[416,512]{1,0:T(8,128)(2,1)} %copy-done.2, ...), custom_call_target="tpu_custom_call" | custom-call | flops 8999999488 | bytes 25000000 | tf_op jit(solution)/shard_map/middle/pallas_call | solution.py:1062
  173.1 15.6 %weight_grad.1 = (bf16[1664,1024]{1,0:T(8,128)(2,1)}, bf16[1152,1024]{1,0:T(8,128)(2,1)}, bf16[512,1024]{1,0:T(8,128)(2,1)}) custom-call(s32[3]{0:T(128)} %pad_add_fusion.meta, bf16[1024,3328]{1,0:T(8,128)(2,1)} %pool_bins.1.pooled_hbm.pooled_ref, bf16[1024,1024]{1,0:T(8,128)(2,1)} %get-tuple-element.72.grad_ref), custom_call_target="tpu_custom_call" | custom-call | flops 7000000000 | bytes 16000000 | tf_op jit(solution)/shard_map/weight_grad/pallas_call | solution.py:1173
  188.7 1.2 collective-permute-start.1
  189.8 61.0 %spread_bins.1.cells_hbm = bf16[21760,128]{1,0:T(8,128)(2,1)} custom-call(s32[17]{0:T(128)} %convert_reduce_fusion.1.starts, s32[32]{0:T(128)} %reshape.372.lows, bf16[1024,1024]{1,0:T(8,128)(2,1)} %get-tuple-element.72.grad_ref, bf16[3328,1024]{1,0:T(8,128)(2,1)} %get-tuple-element.78.weight_hbm, f32[64,512]{1,0:T(8,128)} %pad.34.row_ref, ...), custom_call_target="tpu_custom_call" | custom-call | flops 40000000000 | bytes 15000000 | tf_op jit(solution)/shard_map/spread_bins/pallas_call | solution.py:359
  250.8 1.4 collective-permute-done.1.swapped_hbm
  252.3 1.4 copy-done.11
  253.7 78.3 %reduce_home.1 = (bf16[1664,256]{1,0:T(8,128)(2,1)}, f32[128,256]{1,0:T(8,128)}, f32[1280,128]{1,0:T(8,128)}, f32[5440,128]{1,0:T(8,128)}, bf16[5440,128]{1,0:T(8,128)(2,1)}) custom-call(bf16[1664,1024]{1,0:T(8,128)(2,1)} %get-tuple-element.73.here_hbm, bf16[1152,1024]{1,0:T(8,128)(2,1)} %copy-done.11, bf16[512,1024]{1,0:T(8,128)(2,1)} %get-tuple-element.75.later_hbm, ...), custom_call_target="tpu_custom_call" | custom-call | flops 60000002048 | bytes 200000000 | tf_op jit(solution)/shard_map/reduce_home/pallas_call | solution.py:1593
  332.1 13.5 %finish.1 = (f32[1568,256]{1,0:T(8,128)}, f32[1568,256]{1,0:T(8,128)}, f32[1568,256]{1,0:T(8,128)}, f32[5440,256]{1,0:T(8,128)}, f32[128,256]{1,0:T(8,128)}, /*i...) custom-call(s32[392]{0:T(512)} %constant.216.clone.table, ...), custom_call_target="tpu_custom_call" | custom-call | tf_op jit(solution)/shard_map/finish/pallas_call | solution.py:1749
  345.6 2.0 copy.123
  347.6 2.0 copy.124
  349.6 2.0 copy.125
  351.6 0.9 slice.193
  (124 shorter events, 17.1 us)
Async XLA Ops:
  7.2 10.7 %copy-start.10 = (s32[2,4]{1,0:T(2,128)S(1)}, s32[2,4]{1,0:T(2,128)}, u32[]{:S(2)}) copy-start(s32[2,4]{1,0:T(2,128)} %param.26) | copy-start | bytes 100
  7.2 10.8 %copy-start.5 = (f32[2133]{0:T(1024)S(1)}, f32[2133]{0:T(1024)}, u32[]{:S(2)}) copy-start(f32[2133]{0:T(1024)} %param.37) | copy-start | bytes 25600
  7.2 10.9 %copy-start = (f32[1024,85]{0,1:T(8,128)S(1)}, f32[1024,85]{0,1:T(8,128)}, u32[]{:S(2)}) copy-start(f32[1024,85]{0,1:T(8,128)} %param.34) | copy-start | bytes 1044484
  7.2 12.5 %copy-start.1 = (f32[128,256]{1,0:T(8,128)S(1)}, f32[128,256]{1,0:T(8,128)}, u32[]{:S(2)}) copy-start(f32[128,256]{1,0:T(8,128)} %second_refs_0.1) | copy-start | bytes 393220
  7.2 13.3 %copy-start.3 = (f32[1024,85]{0,1:T(8,128)S(1)}, f32[1024,85]{0,1:T(8,128)}, u32[]{:S(2)}) copy-start(f32[1024,85]{0,1:T(8,128)} %param.35) | copy-start | bytes 1044484
  7.2 14.4 %copy-start.4 = (f32[1024,85]{0,1:T(8,128)S(1)}, f32[1024,85]{0,1:T(8,128)}, u32[]{:S(2)}) copy-start(f32[1024,85]{0,1:T(8,128)} %param.36) | copy-start | bytes 1044484
  13.6 15.5 %all-to-all-start = ((bf16[4,448,256]{2,1,0:T(8,128)(2,1)}), bf16[4,448,256]{2,1,0:T(8,128)(2,1)S(1)}, u32[]{:S(2)}, u32[]{:S(2)}) async-start(bf16[4,448,256]{2,1,0:T(8,128)(2,1)} %deal_rows.1), calls=%async_computation | async-start | bytes 1835008 | tf_op jit(solution)/shard_map/all_to_all | solution.py:484
  17.9 83.3 %all-gather.2.cloned.1.call-start = ((), (), s32[]{:S(2)}) async-start(), calls=%async_computation.2 | async-start | bytes 4423680 | tf_op jit(solution)/shard_map/all_gather | solution.py:493
  23.0 10.1 %copy-start.7 = (f32[8,1024]{1,0:T(8,128)}, f32[8,1024]{1,0:T(8,128)S(1)}, u32[]{:S(2)}) copy-start(f32[8,1024]{1,0:T(8,128)S(1)} %scatter.14.bias_ref) | copy-start | bytes 98308
  30.2 57.9 %copy-start.2 = (bf16[416,512]{1,0:T(8,128)(2,1)}, bf16[416,512]{1,0:T(8,128)(2,1)S(1)}, u32[]{:S(2)}) copy-start(bf16[416,512]{1,0:T(8,128)(2,1)S(1)} %get-tuple-element.163.behind_hbm) | copy-start | bytes 1277956
  31.1 221.2 %reduce-scatter.2.cloned.1.call-start = ((), (), s32[]{:S(2)}) async-start(), calls=%async_computation.3 | async-start | bytes 2359296 | tf_op jit(solution)/shard_map/reduce_scatter | solution.py:1837
  33.5 59.9 %collective-permute-start = (bf16[416,512]{1,0:T(8,128)(2,1)S(1)}, bf16[416,512]{1,0:T(8,128)(2,1)S(1)}, u32[]{:S(2)}, u32[]{:S(2)}) collective-permute-start(bf16[416,512]{1,0:T(8,128)(2,1)S(1)} %get-tuple-element.163.behind_hbm), channel_id=1, source_target_pairs={{0,4},{4,0},{8,12},{12,8},{16,20},{20,16},{24,28},{28,24},{1,5},{5... | collective-permute-start | bytes 1277960 | tf_op jit(solution)/shard_map/ppermute | solution.py:495
  93.4 7.8 %copy-start.12 = (bf16[416,512]{1,0:T(8,128)(2,1)}, bf16[416,512]{1,0:T(8,128)(2,1)S(1)}, u32[]{:S(2)}) copy-start(bf16[416,512]{1,0:T(8,128)(2,1)S(1)} %collective-permute-done.swapped_hbm) | copy-start | bytes 1277956
  188.7 63.6 %collective-permute-start.1 = (bf16[1152,1024]{1,0:T(8,128)(2,1)}, bf16[1152,1024]{1,0:T(8,128)(2,1)S(1)}, u32[]{:S(2)}, u32[]{:S(2)}) collective-permute-start(bf16[1152,1024]{1,0:T(8,128)(2,1)} %get-tuple-element.74), channel_id=1, source_target_pairs={{0,4},{4,0},{8,12},{12,8},{16,20},{20,16},{24,28},{28,24},{1,5},{5... | collective-permute-start | bytes 7077896 | tf_op jit(solution)/shard_map/ppermute | solution.py:1840
  252.3 1.4 copy-start.11
  332.0 21.0 %copy-start.6 = (f32[2133]{0:T(1024)S(1)}, f32[2133]{0:T(1024)}, u32[]{:S(2)}) copy-start(f32[2133]{0:T(1024)} %param.37) | copy-start | bytes 25600
  332.0 21.0 %copy-start.8 = (f32[2133]{0:T(1024)S(1)}, f32[2133]{0:T(1024)}, u32[]{:S(2)}) copy-start(f32[2133]{0:T(1024)} %param.38) | copy-start | bytes 25600
  332.1 21.0 %copy-start.9 = (f32[2133]{0:T(1024)S(1)}, f32[2133]{0:T(1024)}, u32[]{:S(2)}) copy-start(f32[2133]{0:T(1024)} %param.39) | copy-start | bytes 25600
Sparse Core Ops, SparseCore 0:
  31.2 69.9 all-gather.1
  173.2 70.1 reduce-scatter.1

commit v4 on v1

--- a/solution.py
+++ b/solution.py
@@ -706,14 +706,15 @@
         def _():
             each_copy(shard_copies(dp, down_send, down_recv, 0, dp - 2, True), action)
 
-    def relay_shards(distance, took, action):
+    def relay_shards(distance, took, action, pieces=(0, 1, 2)):
         def pass_on(owner, send, recv, neighbour, goes_on, place):
             coming = shard_copies(owner, send, recv, distance - 1, neighbour)
             aside = shard_copies(owner, y_send, y_recv, place, partner)
             onward = [None] * len(coming)
             if distance < 3:
                 onward = shard_copies(owner, send, recv, distance, neighbour)
-            for came_in, on, over in zip(coming, onward, aside):
+            for piece in pieces:
+                came_in, on, over = coming[piece], onward[piece], aside[piece]
                 each_copy([came_in], took)
                 if on is not None:
 
@@ -731,9 +732,11 @@
         def _():
             pass_on(dp + 2 * distance, down_send, down_recv, dp - 2, z > 0, z + distance)
 
-    def serve(distance):
+    def serve(distance, *pieces):
         if by_groups(n_dp):
-            relay_shards(distance, lambda copy: copy.wait_recv(), lambda copy: copy.start())
+            relay_shards(
+                distance, lambda copy: copy.wait_recv(), lambda copy: copy.start(), pieces
+            )
 
     blocks = second_blocks(ahead_hbm, second_ref, hidden_cols(me), second_sem, n_dp)
     for copy in blocks:
@@ -889,14 +892,16 @@
     steps, sums = first_half_product(0)
     each_copy(early, lambda copy: copy.wait())
     steps[0]()
+    serve(1, 0)
     steps[1]()
-    serve(1)
+    serve(1, 1, 2)
+    serve(2, 0)
     second_across.wait_recv()
     second_forward.start()
     steps[2]()
-    serve(2)
+    serve(2, 1, 2)
     steps[3]()
-    serve(3)
+    serve(3, 0, 1, 2)
     each_copy(late, lambda copy: copy.wait())
     if by_groups(n_dp):
         for place in range(4):

time: 358 us -> 356 us (level)
  no operation moved by 1% of the time
where the time goes in v4:
time: 356 us; the launch traced here: 353 us
  Pallas kernels  290 us (81%)
  waiting for transfers between devices  16.2 us (5%)
  between operations  14.6 us (4%)
  other arithmetic  12.5 us (4%)
  local copies, waits for them, and re-layouts  12 us (3%)
  starting transfers between devices  5.57 us (2%)
    pallas_call x1, Pallas kernels, reduce_home(): pl.pallas_call(functools.partial(reduce_kernel, n_dp), out_shape=(jax.Sha...  77.6 us
    pallas_call x1, Pallas kernels, middle(): pl.pallas_call(functools.partial(middle_kernel, n_dp), out_shape=(jax.Sha...  70.7 us
    pallas_call x1, Pallas kernels, spread(): pl.pallas_call(spread_kernel, out_shape=jax.ShapeDtypeStruct((cells, HALF...  61.7 us
    pallas_call x1, Pallas kernels, pool(): pl.pallas_call(pool_kernel, out_shape=jax.ShapeDtypeStruct((count, KQ), j...  51.1 us
    pallas_call x1, Pallas kernels, weight_grad(): pl.pallas_call(functools.partial(weight_grad_kernel, n_dp), grid=(SLOTS /...  15.6 us
    pallas_call x1, Pallas kernels, finish(): pl.pallas_call(finish_kernel, grid=(steps,), out_shape=(shape, shape, sha...  10.9 us
    all_to_all x1, waiting for transfers between devices, gather_quarter(): lax.all_to_all(dealt, 'blk', split_axis=0, concat_axis=0, tiled=True)  7.8 us
    all_gather x1, waiting for transfers between devices, gather_quarter(): gathered = lax.all_gather(ahead, 'dp', axis=0, tiled=True)  7.5 us
  transfers between devices with their start and end apart: 5, of which 3 were waited for; matrix products, arithmetic and copies ran while one was open for 4% of the time, Pallas kernels for 36%

profile of v4, /device:TPU:7, one launch (start us, length us, event | category | flops | bytes accessed | tf_op | source)
XLA Modules:
  0.0 353.2 jit_solution(12031950467425866222)
XLA Ops:
  10.7 2.9 deal_rows.1
  13.5 4.3 %all-to-all-start = ((bf16[4,448,256]{2,1,0:T(8,128)(2,1)}), bf16[4,448,256]{2,1,0:T(8,128)(2,1)S(1)}, u32[]{:S(2)}, u32[]{:S(2)}) async-start(bf16[4,448,256]{2,1,0:T(8,128)(2,1)} %deal_rows.1), calls=%async_computation | async-start | bytes 1835008 | tf_op jit(solution)/shard_map/all_to_all | solution.py:484
  19.9 0.8 pad.33.predict_ref
  21.2 7.8 %all-to-all-done = bf16[4,448,256]{2,1,0:T(8,128)(2,1)S(1)} async-done(((bf16[4,448,256]{2,1,0:T(8,128)(2,1)}), bf16[4,448,256]{2,1,0:T(8,128)(2,1)S(1)}, u32[]{:S(2)}, u32[]{:S(2)}) %all-to-all-start) | async-done | bytes 917536 | tf_op jit(solution)/shard_map/all_to_all | solution.py:484
  29.1 0.8 convert_reduce_fusion
  30.2 0.9 pad_maximum_fusion
  31.1 1.9 fusion.2
  35.9 0.9 maximum_minimum_fusion.1
  36.8 1.0 select_maximum_fusion.uv_ref
  37.9 51.1 %pool_bins.1.pooled_hbm.pooled_ref = bf16[1024,3328]{1,0:T(8,128)(2,1)} custom-call(s32[17]{0:T(128)} %convert_reduce_fusion.1.starts, s32[32]{0:T(128)} %reshape.375.lows, s32[3]{0:T(128)} %pad_add_fusion.meta, bf16[21760,256]{1,0:T(8,128)(2,1)} %feat_hbm.1, f32[1024,128]{1,0:T(8,128)} %select_maximum_fusion.uv_ref), custom_call_target="tpu_custom_call" | custom-call | flops 40000000000 | bytes 13000000 | tf_op jit(solution)/shard_map/pool_bins/pallas_call | solution.py:236
  92.0 0.9 concatenate.25.aux_ref
  93.5 7.5 %all-gather.2.cloned.1.call-done.ahead_hbm = bf16[3840,512]{1,0:T(8,128)(2,1)} async-done(((bf16[480,512]{1,0:T(8,128)(2,1)}), bf16[3840,512]{1,0:T(8,128)(2,1)}) %all-gather.2.cloned.1.call-update) | async-done | bytes 3932176 | tf_op jit(solution)/shard_map/all_gather | solution.py:493
  101.0 1.2 broadcast_in_dim.39.valid_ref
  102.2 70.7 %middle.1 = (bf16[1024,1024]{1,0:T(8,128)(2,1)}, bf16[1024,1024]{1,0:T(8,128)(2,1)}, f32[4,8,40,128]{3,2,1,0:T(8,128)}, bf16[3328,1024]{1,0:T(8,128)(2,1)}) custom-call(bf16[1024,3328]{1,0:T(8,128)(2,1)} %pool_bins.1.pooled_hbm.pooled_ref, bf16[3840,512]{1,0:T(8,128)(2,1)} %all-gather.2.cloned.1.call-done.ahead_hbm, bf16[416,512]{1,0:T(8,128)(2,1)} %copy-done.4, ...), custom_call_target="tpu_custom_call" | custom-call | flops 8999999488 | bytes 25000000 | tf_op jit(solution)/shard_map/middle/pallas_call | solution.py:1067
  173.0 15.6 %weight_grad.1 = (bf16[1664,1024]{1,0:T(8,128)(2,1)}, bf16[1152,1024]{1,0:T(8,128)(2,1)}, bf16[512,1024]{1,0:T(8,128)(2,1)}) custom-call(s32[3]{0:T(128)} %pad_add_fusion.meta, bf16[1024,3328]{1,0:T(8,128)(2,1)} %pool_bins.1.pooled_hbm.pooled_ref, bf16[1024,1024]{1,0:T(8,128)(2,1)} %get-tuple-element.66.grad_ref), custom_call_target="tpu_custom_call" | custom-call | flops 7000000000 | bytes 16000000 | tf_op jit(solution)/shard_map/weight_grad/pallas_call | solution.py:1178
  188.6 1.1 collective-permute-start.1
  189.7 61.7 %spread_bins.1.cells_hbm = bf16[21760,128]{1,0:T(8,128)(2,1)} custom-call(s32[17]{0:T(128)} %convert_reduce_fusion.1.starts, s32[32]{0:T(128)} %reshape.375.lows, bf16[1024,1024]{1,0:T(8,128)(2,1)} %get-tuple-element.66.grad_ref, bf16[3328,1024]{1,0:T(8,128)(2,1)} %get-tuple-element.72.weight_hbm, f32[64,512]{1,0:T(8,128)} %pad.34.row_ref, ...), custom_call_target="tpu_custom_call" | custom-call | flops 40000000000 | bytes 15000000 | tf_op jit(solution)/shard_map/spread_bins/pallas_call | solution.py:359
  251.4 0.9 collective-permute-done.1.swapped_hbm
  252.3 77.6 %reduce_home.1 = (bf16[1664,256]{1,0:T(8,128)(2,1)}, f32[128,256]{1,0:T(8,128)}, f32[1280,128]{1,0:T(8,128)}, f32[5440,128]{1,0:T(8,128)}, bf16[5440,128]{1,0:T(8,128)(2,1)}) custom-call(bf16[1664,1024]{1,0:T(8,128)(2,1)} %get-tuple-element.67.here_hbm, bf16[1152,1024]{1,0:T(8,128)(2,1)} %collective-permute-done.1.swapped_hbm, ...), custom_call_target="tpu_custom_call" | custom-call | flops 60000002048 | bytes 200000000 | tf_op jit(solution)/shard_map/reduce_home/pallas_call | solution.py:1598
  330.0 1.2 slice.203
  331.1 0.9 slice.201
  333.5 1.1 multiply_subtract_fusion
  334.7 0.8 multiply_subtract_fusion.1
  335.5 10.9 %finish.1 = (f32[1568,256]{1,0:T(8,128)}, f32[1568,256]{1,0:T(8,128)}, f32[1568,256]{1,0:T(8,128)}, f32[5440,256]{1,0:T(8,128)}) custom-call(s32[392]{0:T(512)} %constant.240.clone.table, bf16[1664,256]{1,0:T(8,128)(2,1)} %get-tuple-element.73.home_ref, f32[1568,256]{1,0:T(8,128)} %weight_ref.3, f32[1568,256]{1,0:T(8,128)} %mean_ref.1, ...), custom_call_target="tpu_custom_call" | custom-call | tf_op jit(solution)/shard_map/finish/pallas_call | solution.py:1708
  (130 shorter events, 14.2 us)
Async XLA Ops:
  7.2 10.7 %copy-start.15 = (s32[2,4]{1,0:T(2,128)S(1)}, s32[2,4]{1,0:T(2,128)}, u32[]{:S(2)}) copy-start(s32[2,4]{1,0:T(2,128)} %param.26) | copy-start | bytes 100
  7.2 10.8 %copy-start.10 = (f32[2133]{0:T(1024)S(1)}, f32[2133]{0:T(1024)}, u32[]{:S(2)}) copy-start(f32[2133]{0:T(1024)} %param.37) | copy-start | bytes 25600
  7.2 11.5 %copy-start.2 = (f32[128,256]{1,0:T(8,128)S(1)}, f32[128,256]{1,0:T(8,128)}, u32[]{:S(2)}) copy-start(f32[128,256]{1,0:T(8,128)} %param.31) | copy-start | bytes 393220
  7.2 11.6 %copy-start = (f32[1024,85]{0,1:T(8,128)S(1)}, f32[1024,85]{0,1:T(8,128)}, u32[]{:S(2)}) copy-start(f32[1024,85]{0,1:T(8,128)} %param.34) | copy-start | bytes 1044484
  13.5 15.5 %all-to-all-start = ((bf16[4,448,256]{2,1,0:T(8,128)(2,1)}), bf16[4,448,256]{2,1,0:T(8,128)(2,1)S(1)}, u32[]{:S(2)}, u32[]{:S(2)}) async-start(bf16[4,448,256]{2,1,0:T(8,128)(2,1)} %deal_rows.1), calls=%async_computation | async-start | bytes 1835008 | tf_op jit(solution)/shard_map/all_to_all | solution.py:484
  17.9 83.2 %all-gather.2.cloned.1.call-start = ((), (), s32[]{:S(2)}) async-start(), calls=%async_computation.2 | async-start | bytes 4423680 | tf_op jit(solution)/shard_map/all_gather | solution.py:493
  19.8 13.2 %copy-start.12 = (f32[8,1024]{1,0:T(8,128)}, f32[8,1024]{1,0:T(8,128)S(1)}, u32[]{:S(2)}) copy-start(f32[8,1024]{1,0:T(8,128)S(1)} %scatter.14.bias_ref) | copy-start | bytes 98308
  30.1 58.8 %copy-start.4 = (bf16[416,512]{1,0:T(8,128)(2,1)}, bf16[416,512]{1,0:T(8,128)(2,1)S(1)}, u32[]{:S(2)}) copy-start(bf16[416,512]{1,0:T(8,128)(2,1)S(1)} %get-tuple-element.129.behind_hbm) | copy-start | bytes 1277956
  31.0 221.3 %reduce-scatter.2.cloned.1.call-start = ((), (), s32[]{:S(2)}) async-start(), calls=%async_computation.3 | async-start | bytes 2359296 | tf_op jit(solution)/shard_map/reduce_scatter | solution.py:1788
  33.4 60.1 %collective-permute-start = (bf16[416,512]{1,0:T(8,128)(2,1)S(1)}, bf16[416,512]{1,0:T(8,128)(2,1)S(1)}, u32[]{:S(2)}, u32[]{:S(2)}) collective-permute-start(bf16[416,512]{1,0:T(8,128)(2,1)S(1)} %get-tuple-element.129.behind_hbm), channel_id=1, source_target_pairs={{0,4},{4,0},{8,12},{12,8},{16,20},{20,16},{24,28},{28,24},{1,5},{5... | collective-permute-start | bytes 1277960 | tf_op jit(solution)/shard_map/ppermute | solution.py:495
  93.5 8.7 %copy-start.16 = (bf16[416,512]{1,0:T(8,128)(2,1)}, bf16[416,512]{1,0:T(8,128)(2,1)S(1)}, u32[]{:S(2)}) copy-start(bf16[416,512]{1,0:T(8,128)(2,1)S(1)} %collective-permute-done.swapped_hbm) | copy-start | bytes 1277956
  188.6 63.7 %collective-permute-start.1 = (bf16[1152,1024]{1,0:T(8,128)(2,1)}, bf16[1152,1024]{1,0:T(8,128)(2,1)}, u32[]{:S(2)}, u32[]{:S(2)}) collective-permute-start(bf16[1152,1024]{1,0:T(8,128)(2,1)} %get-tuple-element.68), channel_id=1, source_target_pairs={{0,4},{4,0},{8,12},{12,8},{16,20},{20,16},{24,28},{28,24},{1,5},{5... | collective-permute-start | bytes 7077896 | tf_op jit(solution)/shard_map/ppermute | solution.py:1791
  252.3 80.5 %copy-start.11 = (f32[2133]{0:T(1024)S(1)}, f32[2133]{0:T(1024)}, u32[]{:S(2)}) copy-start(f32[2133]{0:T(1024)} %param.37) | copy-start | bytes 25600
  252.3 80.5 %copy-start.13 = (f32[2133]{0:T(1024)S(1)}, f32[2133]{0:T(1024)}, u32[]{:S(2)}) copy-start(f32[2133]{0:T(1024)} %param.38) | copy-start | bytes 25600
  252.3 80.6 %copy-start.14 = (f32[2133]{0:T(1024)S(1)}, f32[2133]{0:T(1024)}, u32[]{:S(2)}) copy-start(f32[2133]{0:T(1024)} %param.39) | copy-start | bytes 25600
  252.3 81.2 %copy-start.1 = (f32[1024,85]{0,1:T(8,128)S(1)}, f32[1024,85]{0,1:T(8,128)}, u32[]{:S(2)}) copy-start(f32[1024,85]{0,1:T(8,128)} %param.34) | copy-start | bytes 1044484
  252.3 81.2 %copy-start.5 = (f32[1024,85]{0,1:T(8,128)S(1)}, f32[1024,85]{0,1:T(8,128)}, u32[]{:S(2)}) copy-start(f32[1024,85]{0,1:T(8,128)} %param.35) | copy-start | bytes 1044484
  252.3 81.2 %copy-start.6 = (f32[1024,85]{0,1:T(8,128)S(1)}, f32[1024,85]{0,1:T(8,128)}, u32[]{:S(2)}) copy-start(f32[1024,85]{0,1:T(8,128)} %param.36) | copy-start | bytes 1044484
  329.9 4.7 %copy-start.3 = (f32[128,256]{1,0:T(8,128)S(1)}, f32[128,256]{1,0:T(8,128)}, u32[]{:S(2)}) copy-start(f32[128,256]{1,0:T(8,128)} %param.31) | copy-start | bytes 393220
  329.9 4.7 %copy-start.7 = (f32[128,256]{1,0:T(8,128)S(1)}, f32[128,256]{1,0:T(8,128)}, u32[]{:S(2)}) copy-start(f32[128,256]{1,0:T(8,128)} %param.32) | copy-start | bytes 393220
  329.9 4.7 %copy-start.8 = (f32[128,256]{1,0:T(8,128)S(1)}, f32[128,256]{1,0:T(8,128)}, u32[]{:S(2)}) copy-start(f32[128,256]{1,0:T(8,128)} %param.33) | copy-start | bytes 393220
  330.0 4.7 %copy-start.9 = (f32[128,256]{1,0:T(8,128)S(1)}, f32[128,256]{1,0:T(8,128)}, u32[]{:S(2)}) copy-start(f32[128,256]{1,0:T(8,128)} %get-tuple-element.81) | copy-start | bytes 393220
Sparse Core Ops, SparseCore 0:
  31.2 69.7 all-gather.1
  173.1 71.6 reduce-scatter.1
